TPU v7x, 256 devices: a whole 4x4x8 slice. The times are simulated.
256 devices in a mesh: lon: 16 (over x_hi, y, core), lat: 8 (over z), comp: 2 (over x_lo).
Axes of the slice: x: 4 (x_hi: 2, x_lo: 2; x = x_hi * 2 + x_lo), y: 4, z: 8, core: 2. Of those that a mesh axis runs over, the one named last changes fastest.
Arguments:
- state: float32 [2, 2, 64, 128, 4096], P('comp', None, None, 'lat', 'lon'), may hold values from -6 to 6
- params: float32 [2, 3, 2, 128, 4096], P('comp', None, None, 'lat', 'lon'), may hold values from -2 to 10, as said below
- couple_weight: float32 [2, 8, 2, 64], P('comp'), may hold values from -0.5 to 0.5
- weight_table: float32 [2, 4, 2], P('comp'), may hold values from 0.2 to 0.8
- intersection_map: int32 [2, 128, 4096], P('comp', 'lat', 'lon'), may hold values from 0 to 15
- sea_mask: int32 [2, 128, 4096], P('comp', 'lat', 'lon'), may hold values 0 or 1
Outputs:
- new_state: float32 [2, 2, 64, 128, 4096], P('comp', None, None, 'lat', 'lon')
- coupled: float32 [2, 8, 128, 4096], P('comp', None, 'lat', 'lon')
Inputs may be any that keep to these rules, and one draw needn't show every extreme that they name: `params`: along dimension 1: horizontal diffusion numbers from 0.03 to 0.24, vertical diffusion numbers from 0.1 to 10, surface forcing from -2 to 2.
All inputs are finite; a program needn't handle non-finite values. No bound on the sum of `sea_mask` on one device may be relied on, other than what follows from the above.
Results may differ from a plain program's by a relative error of at most 0.0001.
Values sent between devices are 32-bit elements; how exact they have to be, the bound alone decides.
No kernel may reach another device: no remote copies, remote signals or barrier semaphores. Data moves between devices by JAX's collectives and lax.ppermute only.
A program may use at most 128 MiB of HBM per device.

v0:
```python
import jax
import jax.numpy as jnp
from jax import lax
from jax.experimental import pallas as pl
from jax.experimental.pallas import tpu as pltpu
from jax.sharding import PartitionSpec as P

STEPS = 4
LEV = 64
HALF = LEV // 2
ROWS = 16
HALO = 4
COLS = 256
NQ = 8
OFF = 8
TALL = 32
PLANES = LEV + 3
STRIPS = HALF // 2 + 2
VMEM = pl.BlockSpec(memory_space=pltpu.VMEM)
SMEM = pl.BlockSpec(memory_space=pltpu.SMEM)
HBM = pl.BlockSpec(memory_space=pltpu.HBM)
BF16 = jnp.bfloat16
F32 = jnp.float32


def lanes():
    return lax.broadcasted_iota(jnp.int32, (8, 128), 1)


def subs():
    return lax.broadcasted_iota(jnp.int32, (8, 128), 0)


def level_of(level, h):
    return level if h == 0 else LEV - 1 - level


def halves(value):
    high = value.astype(BF16)
    return high, (value - high.astype(F32)).astype(BF16)


def params_of(vmem):
    return pltpu.CompilerParams(vmem_limit_bytes=vmem * 2**20)


def roll(value, shift):
    return pltpu.roll(value, shift % 128, 1)


def load_kernel(state, params, x0, strips, near, sem, near_sem):
    lane = lanes()
    part = LEV // 4
    copies = {}
    for n in (0, 3, 1, 2):
        for f in range(2):
            for c in range(2):
                copies[n, f, c] = pltpu.make_async_copy(
                    state.at[0, f, pl.ds(part * n, part), :, pl.ds(128 * c, 128)],
                    x0.at[f, pl.ds(part * n, part), c, pl.ds(OFF, ROWS)],
                    sem.at[n, f, c],
                )
                copies[n, f, c].start()
    small = pltpu.make_async_copy(params.at[0], near, near_sem)
    small.start()

    def place(total, source, index):
        ring = jnp.where(lane >= 124, source[1], source[0])
        first = roll(ring, 16 * index + 4)
        second = roll(ring, 16 * index + 12)
        inside = (lane >= 16 * index) & (lane < 16 * index + 16)
        pair = jnp.where((lane & 8) == 0, first, second)
        return pair if total is None else jnp.where(inside, pair, total)

    def strip(block, carry):
        for rt in range(2):
            at = OFF + 8 * rt
            total = None
            for lq in range(2):
                for f in range(2):
                    for h in range(2):
                        lam = level_of(block * 2 + lq, h)
                        source = [x0[f, lam, c, at:at + 8] for c in range(2)]
                        total = place(total, source, lq * 4 + f * 2 + h)
            strips[block, 8 * rt:8 * rt + 8] = total
        return carry

    for n in range(2):
        for m in (n, 3 - n):
            for f in range(2):
                for c in range(2):
                    copies[m, f, c].wait()
        lax.fori_loop(n * part // 2, (n + 1) * part // 2, strip, 0)
    small.wait()
    for rt in range(2):
        rows = slice(8 * rt, 8 * rt + 8)
        total = None
        for lq in range(2):
            for f in range(2):
                for h in range(2):
                    source = [near[lq, f, rows, 128 * c:128 * c + 128] for c in range(2)]
                    total = place(total, source, lq * 4 + f * 2 + h)
        strips[HALF // 2, rows] = total
        total = jnp.zeros((8, 128), F32)
        for f in range(2):
            source = [near[2, f, rows, 128 * c:128 * c + 128] for c in range(2)]
            total = place(total, source, f * 2)
        strips[HALF // 2 + 1, rows] = total


def join_kernel(strips, west, east, low_in, high_in, joined, low_rows, high_rows):
    place = lanes() & 15
    for block in range(STRIPS):
        for rt in range(2):
            rows = slice(8 * rt, 8 * rt + 8)
            joined[block, rows] = jnp.where(
                place < 4, west[block, rows], jnp.where(place >= 12, east[block, rows], strips[block, rows])
            )
        cols = slice(128 * (block % 2), 128 * (block % 2) + 128)
        low_rows[2 * PLANES + block // 2, :, cols] = joined[block, 0:HALO]
        high_rows[2 * PLANES + block // 2, :, cols] = joined[block, ROWS - HALO:ROWS]


def kron_weights(couple_weight, out, rows):
    width = HALF * rows
    level = lax.broadcasted_iota(jnp.int32, (LEV, width), 0)
    place = lax.broadcasted_iota(jnp.int32, (LEV, width), 1)
    spread = []
    for h in range(2):
        first = rows * level_of(level, h)
        spread.append(((place >= first) & (place < first + rows)).astype(F32).astype(BF16))
    row = lax.broadcasted_iota(jnp.int32, (rows, width), 0)
    within = lax.broadcasted_iota(jnp.int32, (rows, width), 1) & (rows - 1)
    keep = within == row
    for f in range(2):
        for n, part in enumerate(halves(couple_weight[0, :, f, :])):
            for h in range(2):
                wide = jnp.dot(part, spread[h], preferred_element_type=F32)
                for q in range(0, NQ, 2):
                    at = n * NQ * rows + q * rows
                    pair = [jnp.where(keep, wide[q + i:q + i + 1], 0.0) for i in range(2)]
                    out[f, h, at:at + 2 * rows] = jnp.concatenate(pair, axis=0).astype(BF16)


def prepare_kernel(x0, params, couple_weight,
                   low_rows, high_rows, weights, narrow, sides, strip_sides, par, coef, xhi, xlo):
    def some(level, carry):
        at = pl.ds(pl.multiple_of(level * ROWS, 16), ROWS)
        for f in range(2):
            for h in range(2):
                lam = level_of(level, h)
                for c in range(2):
                    cols = slice(128 * c, 128 * c + 128)
                    value = x0[f, lam, c, OFF:OFF + ROWS]
                    high, low = halves(value)
                    xhi[f, h, at, cols] = high
                    xlo[f, h, at, cols] = low
                    low_rows[f * PLANES + lam, :, cols] = x0[f, lam, c, OFF:OFF + HALO]
                    high_rows[f * PLANES + lam, :, cols] = x0[f, lam, c, OFF + ROWS - HALO:OFF + ROWS]
        return carry

    for f in range(2):
        for kind in range(3):
            low_rows[f * PLANES + LEV + kind] = params[0, kind, f, 0:HALO]
            high_rows[f * PLANES + LEV + kind] = params[0, kind, f, ROWS - HALO:ROWS]
    columns = [(f, c, rt) for f in range(2) for c in range(2) for rt in range(2)]
    for f, c, rt in columns:
        rows = slice(8 * rt, 8 * rt + 8)
        h, k, g = [params[0, kind, f, rows, 128 * c:128 * c + 128] for kind in range(3)]
        for n, value in enumerate((h, k, g, 1.0 / k, 1.0 - 4.0 * h)):
            par[n, f, c, rows] = value

    def pivots(level, carry):
        out = []
        for n, (f, c, rt) in enumerate(columns):
            rows = slice(8 * rt, 8 * rt + 8)
            k = par[1, f, c, rows]
            m = k / (1.0 + 2.0 * k - k * carry[n])
            coef[f, level, c, rows] = m
            out.append(m)
        some(level, 0)
        return tuple(out)

    last = lax.fori_loop(0, HALF, pivots, (jnp.ones((8, 128), F32),) * len(columns))
    for n, (f, c, rt) in enumerate(columns):
        coef[f, HALF, c, 8 * rt:8 * rt + 8] = last[n] / (1.0 - last[n] * last[n])
    kron_weights(couple_weight, weights, ROWS)
    kron_weights(couple_weight, narrow, 8)
    row = lax.broadcasted_iota(jnp.int32, (COLS, COLS), 0)
    col = lax.broadcasted_iota(jnp.int32, (COLS, COLS), 1)
    inner = (jnp.abs(row - col) == 1).astype(F32).astype(jnp.bfloat16)
    lane = row & 127
    for f in range(2):
        for h in range(2):
            base = f * 32 + h * 16
            rim = ((lane == base + 3) & (col == 0)) | ((lane == base + 12) & (col == COLS - 1))
            sides[f, h, 0:COLS] = inner
            sides[f, h, COLS:2 * COLS] = inner
            sides[f, h, 2 * COLS:3 * COLS] = rim.astype(F32).astype(jnp.bfloat16)
    near = jnp.abs((row & 127) - col)[:, 0:128] == 1
    strip_sides[...] = near.astype(F32).astype(jnp.bfloat16)

def strip_params(spar):
    for rt in range(2):
        rows = slice(8 * rt, 8 * rt + 8)
        k = spar[1, rows]
        k = jnp.where(k > 0.0, k, 1.0)
        spar[1, rows] = k
        spar[3, rows] = 1.0 / k
        spar[4, rows] = 1.0 - 4.0 * spar[0, rows]


def strip_pivots(spar, scoef, level, carry):
    out = []
    for rt in range(2):
        rows = slice(8 * rt, 8 * rt + 8)
        k = spar[1, rows]
        m = k / (1.0 + 2.0 * k - k * carry[rt])
        scoef[level, rows] = m
        out.append(m)
    return tuple(out)


def strip_closing(scoef, last):
    for rt in range(2):
        scoef[HALF, 8 * rt:8 * rt + 8] = last[rt] / (1.0 - last[rt] * last[rt])


def swap_ends(value):
    return jnp.where((lanes() & 16) == 0, roll(value, -16), roll(value, 16))


def inner_kernel(strips, x0_in, xhi_in, xlo_in, par, coef, weights, sides, strip_sides,
                 x0, xhi, xlo, x1, x2, x3, x4, t0, t1, t2, t3, sums,
                 xe, te, spar, scoef, tsplit, beside, strip_beside):
    xs, ts = (x0, x1, x2, x3, x4), (t0, t1, t2, t3)
    sub = subs()
    zero = jnp.zeros((8, 128), F32)

    for rt in range(2):
        rows = slice(8 * rt, 8 * rt + 8)
        spar[0, rows] = strips[HALF // 2, rows]
        spar[1, rows] = roll(strips[HALF // 2, rows], 64)
        spar[2, rows] = strips[HALF // 2 + 1, rows]
    strip_params(spar)

    def unstrip(block, carry):
        for lq in range(2):
            level = block * 2 + lq
            tiles = [roll(strips[block, 8 * rt:8 * rt + 8], 64 * lq) for rt in range(2)]
            for rt in range(2):
                t0[level, OFF + 8 * rt:OFF + 8 * rt + 8] = tiles[rt]
            split_strip(level, tiles)
            carry = strip_pivots(spar, scoef, level, carry)
        return carry

    def split_strip(level, tiles):
        at = pl.ds(pl.multiple_of(level * ROWS, 16), ROWS)
        high, low = halves(jnp.concatenate(tiles, axis=0))
        tsplit[at, 0:128] = high
        tsplit[at, 128:256] = low

    one = jnp.ones((8, 128), F32)
    strip_closing(scoef, lax.fori_loop(0, HALF // 2, unstrip, (one, one)))

    def vertical(load, rt):
        at = OFF + 8 * rt
        up, down = load(at - 1), load(at + 1)
        if rt == 0:
            up = jnp.where(sub == 0, 0.0, up)
        else:
            down = jnp.where(sub == 7, 0.0, down)
        return up + down

    def neighbours():
        def part(i, carry):
            at = pl.ds(pl.multiple_of(i * 256, 16), 256)
            for f in range(2):
                for h in range(2):
                    value = jnp.concatenate([xhi[f, h, at], xlo[f, h, at], tsplit[at]], axis=1)
                    beside[f, h, at] = jnp.dot(value, sides[f, h], preferred_element_type=F32)
            strip_beside[at] = jnp.dot(tsplit[at], strip_sides[...], preferred_element_type=F32)
            return carry

        lax.fori_loop(0, HALF * ROWS // 256, part, 0)

    def packages(n):
        total = None
        for f in range(2):
            for h in range(2):
                both = jnp.dot(weights[f, h], xhi[f, h], preferred_element_type=F32)
                high = jnp.dot(weights[f, h, :NQ * ROWS], xlo[f, h], preferred_element_type=F32)
                value = (both[NQ * ROWS:] + high) + both[:NQ * ROWS]
                total = value if total is None else total + value
        sums[n] = total

    def main_field(x, xn, f):
        tiles = [(c, rt, slice(8 * rt, 8 * rt + 8), OFF + 8 * rt) for c in range(2) for rt in range(2)]
        diff = [par[0, f, c, rows] for c, rt, rows, at in tiles]
        keep = [par[4, f, c, rows] for c, rt, rows, at in tiles]

        def forward(i, carry):
            carry = list(carry)
            for u in range(2):
                level = i * 2 + u
                for n, (c, rt, rows, at) in enumerate(tiles):
                    m = coef[f, level, c, rows]
                    flat = pl.ds(pl.multiple_of(level * ROWS, 8) + 8 * rt, 8)
                    for h in range(2):
                        lam = level_of(level, h)
                        around = vertical(lambda r: x[f, lam, c, r:r + 8], rt)
                        around = around + beside[f, h, flat, 128 * c:128 * c + 128]
                        e = (keep[n] * x[f, lam, c, at:at + 8] + diff[n] * around) + carry[h * 4 + n]
                        xe[lam, c, rows] = e
                        carry[h * 4 + n] = m * e
            return tuple(carry)

        start = tuple(par[2, f, c, rows] for c, rt, rows, at in tiles) + (zero,) * 4
        ends = lax.fori_loop(0, HALF // 2, forward, start)
        inv = [par[3, f, c, rows] for c, rt, rows, at in tiles]

        def finish(level, h, z):
            lam = level_of(level, h)
            flat = pl.ds(pl.multiple_of(level * ROWS, 16), ROWS)
            for c in range(2):
                y = []
                for rt in range(2):
                    v = z[h * 4 + 2 * c + rt] * inv[2 * c + rt]
                    xn[f, lam, c, OFF + 8 * rt:OFF + 8 * rt + 8] = v
                    y.append(v)
                high, low = halves(jnp.concatenate(y, axis=0))
                xhi[f, h, flat, 128 * c:128 * c + 128] = high
                xlo[f, h, flat, 128 * c:128 * c + 128] = low

        z = [None] * 8
        for h in range(2):
            for n, (c, rt, rows, at) in enumerate(tiles):
                z[h * 4 + n] = coef[f, HALF, c, rows] * (xe[HALF - 1 + h, c, rows] + ends[(1 - h) * 4 + n])
        for h in range(2):
            finish(HALF - 1, h, z)

        def back_level(level, z):
            out = [None] * 8
            for h in range(2):
                lam = level_of(level, h)
                for n, (c, rt, rows, at) in enumerate(tiles):
                    out[h * 4 + n] = coef[f, level, c, rows] * (xe[lam, c, rows] + z[h * 4 + n])
                finish(level, h, out)
            return tuple(out)

        def back(i, z):
            for u in range(3):
                z = back_level(HALF - 2 - (i * 3 + u), z)
            return z

        z = lax.fori_loop(0, HALF // 3, back, tuple(z))
        back_level(0, z)

    def strip_step(t, tn):
        tiles = [slice(8 * rt, 8 * rt + 8) for rt in range(2)]
        diff = [spar[0, rows] for rows in tiles]
        inv = [spar[3, rows] for rows in tiles]
        keep = [spar[4, rows] for rows in tiles]

        def forward(i, carry):
            carry = list(carry)
            for u in range(4):
                level = i * 4 + u
                for rt, rows in enumerate(tiles):
                    flat = pl.ds(pl.multiple_of(level * ROWS, 8) + 8 * rt, 8)
                    around = vertical(lambda r: t[level, r:r + 8], rt) + strip_beside[flat]
                    e = (keep[rt] * t[level, OFF + 8 * rt:OFF + 8 * rt + 8] + diff[rt] * around) + carry[rt]
                    te[level, rows] = e
                    carry[rt] = scoef[level, rows] * e
            return tuple(carry)

        ends = lax.fori_loop(0, HALF // 4, forward, tuple(spar[2, rows] for rows in tiles))
        def finish(level, z):
            y = [z[rt] * inv[rt] for rt in range(2)]
            for rt in range(2):
                tn[level, OFF + 8 * rt:OFF + 8 * rt + 8] = y[rt]
            split_strip(level, y)

        z = [scoef[HALF, rows] * (te[HALF - 1, rows] + swap_ends(ends[rt])) for rt, rows in enumerate(tiles)]
        finish(HALF - 1, z)

        def back_level(level, z):
            out = [scoef[level, rows] * (te[level, rows] + z[rt]) for rt, rows in enumerate(tiles)]
            finish(level, out)
            return tuple(out)

        def back(i, z):
            for u in range(3):
                z = back_level(HALF - 2 - (i * 3 + u), z)
            return z

        z = lax.fori_loop(0, HALF // 3, back, tuple(z))
        back_level(0, z)

    for step in range(STEPS):
        neighbours()
        if step > 0:
            packages(step - 1)
        for f in range(2):
            main_field(xs[step], xs[step + 1], f)
        if step < STEPS - 1:
            strip_step(ts[step], ts[step + 1])
    packages(STEPS - 1)


def outer_kernel(below, above, strips, params, sums, narrow, sides, strip_sides,
                 i0, i1, i2, i3, i4, j0, j1, j2, j3,
                 new_state, mean, edges, x0, x1, x2, x3, x4, t0, t1, t2, t3,
                 xe, te, par, coef, spar, scoef, centre, xhi, xlo, tcentre, tsplit, beside, strip_beside, patch, sem):
    xs, ts = (x0, x1, x2, x3, x4), (t0, t1, t2, t3)
    lane, sub = lanes(), subs()
    top = sub < 4
    zero = jnp.zeros((8, 128), F32)

    def strip_rim(ref, block):
        return ref[2 * PLANES + block // 2, :, 128 * (block % 2):128 * (block % 2) + 128]

    for n, (block, shift) in enumerate(((HALF // 2, 0), (HALF // 2, 64), (HALF // 2 + 1, 0))):
        spar[n, 0:4] = pltpu.roll(strip_rim(below, block), shift, 1)
        spar[n, 4:8] = pltpu.roll(strips[block, 0:4], shift, 1)
        spar[n, 8:12] = pltpu.roll(strips[block, 12:16], shift, 1)
        spar[n, 12:16] = pltpu.roll(strip_rim(above, block), shift, 1)
    strip_params(spar)
    columns = [(f, c, rt) for f in range(2) for c in range(2) for rt in range(2)]
    for f in range(2):
        for c in range(2):
            cols = slice(128 * c, 128 * c + 128)
            for n in range(3):
                par[n, f, c, 0:4] = below[f * PLANES + LEV + n, :, cols]
                par[n, f, c, 4:8] = params[0, n, f, 0:4, cols]
                par[n, f, c, 8:12] = params[0, n, f, 12:16, cols]
                par[n, f, c, 12:16] = above[f * PLANES + LEV + n, :, cols]
    for f, c, rt in columns:
        rows = slice(8 * rt, 8 * rt + 8)
        k = par[1, f, c, rows]
        k = jnp.where(k > 0.0, k, 1.0)
        par[1, f, c, rows] = k
        par[3, f, c, rows] = 1.0 / k
        par[4, f, c, rows] = 1.0 - 4.0 * par[0, f, c, rows]

    def pivots(level, carry):
        out = []
        for n, (f, c, rt) in enumerate(columns):
            rows = slice(8 * rt, 8 * rt + 8)
            k = par[1, f, c, rows]
            m = k / (1.0 + 2.0 * k - k * carry[n])
            coef[f, level, c, rows] = m
            out.append(m)
        out.extend(strip_pivots(spar, scoef, level, carry[len(columns):]))
        for f in range(2):
            for h in range(2):
                lam = level_of(level, h)
                for c in range(2):
                    cols = slice(128 * c, 128 * c + 128)
                    x0[f, lam, c, OFF - HALO:OFF] = below[f * PLANES + lam, :, cols]
                    x0[f, lam, c, OFF + ROWS:OFF + ROWS + HALO] = above[f * PLANES + lam, :, cols]
        return tuple(out)

    last = lax.fori_loop(0, HALF, pivots, (jnp.ones((8, 128), F32),) * (len(columns) + 2))
    for n, (f, c, rt) in enumerate(columns):
        coef[f, HALF, c, 8 * rt:8 * rt + 8] = last[n] / (1.0 - last[n] * last[n])
    strip_closing(scoef, last[len(columns):])

    def unstrip(i, carry):
        for c in range(2):
            cols = slice(128 * c, 128 * c + 128)
            for lq in range(2):
                level = i * 4 + c * 2 + lq
                t0[level, OFF - HALO:OFF] = pltpu.roll(below[2 * PLANES + i, :, cols], 64 * lq, 1)
                t0[level, OFF + ROWS:OFF + ROWS + HALO] = pltpu.roll(above[2 * PLANES + i, :, cols], 64 * lq, 1)
        return carry

    lax.fori_loop(0, HALF // 4, unstrip, 0)

    def gather(x, step):
        a, b = OFF - 4 + step, OFF + 12 - step

        def some(i, carry):
            at = pl.ds(pl.multiple_of(i * 16, 16), 16)
            for f in range(2):
                for h in range(2):
                    for c in range(2):
                        pair = []
                        for u in range(2):
                            lam = level_of(i * 2 + u, h)
                            v = jnp.where(top, x[f, lam, c, a:a + 8], x[f, lam, c, b:b + 8])
                            centre[f, lam, c] = v
                            pair.append(v)
                        high, low = halves(jnp.concatenate(pair, axis=0))
                        xhi[f, h, at, 128 * c:128 * c + 128] = high
                        xlo[f, h, at, 128 * c:128 * c + 128] = low
            return carry

        lax.fori_loop(0, HALF // 2, some, 0)

    def gather_strip(t, step):
        a, b = OFF - 4 + step, OFF + 12 - step

        def some(i, carry):
            at = pl.ds(pl.multiple_of(i * 16, 16), 16)
            pair = []
            for u in range(2):
                v = jnp.where(top, t[i * 2 + u, a:a + 8], t[i * 2 + u, b:b + 8])
                tcentre[i * 2 + u] = v
                pair.append(v)
            high, low = halves(jnp.concatenate(pair, axis=0))
            tsplit[at, 0:128] = high
            tsplit[at, 128:256] = low
            return carry

        lax.fori_loop(0, HALF // 2, some, 0)

    def neighbours():
        for f in range(2):
            for h in range(2):
                value = jnp.concatenate([xhi[f, h], xlo[f, h], tsplit[...]], axis=1)
                beside[f, h] = jnp.dot(value, sides[f, h], preferred_element_type=F32)
        strip_beside[...] = jnp.dot(tsplit[...], strip_sides[...], preferred_element_type=F32)

    def packages(n, step):
        a, b = OFF - 4 + step, OFF + 12 - step
        total = None
        for f in range(2):
            for h in range(2):
                both = jnp.dot(narrow[f, h], xhi[f, h], preferred_element_type=F32)
                high = jnp.dot(narrow[f, h, :NQ * 8], xlo[f, h], preferred_element_type=F32)
                value = (both[NQ * 8:] + high) + both[:NQ * 8]
                total = value if total is None else total + value
        for q in range(NQ):
            for c in range(2):
                v = total[q * 8:q * 8 + 8, 128 * c:128 * c + 128]
                pltpu.store(patch.at[n, q, c, pl.ds(a, 8)], v, mask=top)
                pltpu.store(patch.at[n, q, c, pl.ds(b, 8)], v, mask=sub >= 4)

    def main_field(x, xn, f, step):
        a, b = OFF - 4 + step, OFF + 12 - step

        def mine(load):
            return jnp.where(top, load(slice(step, step + 8)), load(slice(8 - step, 16 - step)))

        def put(lam, c, v):
            pltpu.store(xn.at[f, lam, c, pl.ds(a, 8)], v, mask=top)
            pltpu.store(xn.at[f, lam, c, pl.ds(b, 8)], v, mask=sub >= 4)

        diff = [mine(lambda r: par[0, f, c, r]) for c in range(2)]
        keep = [mine(lambda r: par[4, f, c, r]) for c in range(2)]
        inv = [mine(lambda r: par[3, f, c, r]) for c in range(2)]

        def forward(i, carry):
            carry = list(carry)
            for u in range(4):
                level = i * 4 + u
                m = [mine(lambda r: coef[f, level, c, r]) for c in range(2)]
                flat = pl.ds(pl.multiple_of(level * 8, 8), 8)
                for h in range(2):
                    lam = level_of(level, h)
                    for c in range(2):
                        around = jnp.where(
                            top,
                            x[f, lam, c, a - 1:a + 7] + x[f, lam, c, a + 1:a + 9],
                            x[f, lam, c, b - 1:b + 7] + x[f, lam, c, b + 1:b + 9],
                        ) + beside[f, h, flat, 128 * c:128 * c + 128]
                        e = (keep[c] * centre[f, lam, c] + diff[c] * around) + carry[h * 2 + c]
                        xe[lam, c] = e
                        carry[h * 2 + c] = m[c] * e
            return tuple(carry)

        start = (mine(lambda r: par[2, f, 0, r]), mine(lambda r: par[2, f, 1, r]), zero, zero)
        ends = lax.fori_loop(0, HALF // 4, forward, start)
        z = []
        for h in range(2):
            for c in range(2):
                v = mine(lambda r: coef[f, HALF, c, r]) * (xe[HALF - 1 + h, c] + ends[(1 - h) * 2 + c])
                put(HALF - 1 + h, c, v * inv[c])
                z.append(v)

        def back_level(level, z):
            out = []
            m = [mine(lambda r: coef[f, level, c, r]) for c in range(2)]
            for h in range(2):
                lam = level_of(level, h)
                for c in range(2):
                    v = m[c] * (xe[lam, c] + z[h * 2 + c])
                    put(lam, c, v * inv[c])
                    out.append(v)
            return tuple(out)

        def back(i, z):
            for u in range(3):
                z = back_level(HALF - 2 - (i * 3 + u), z)
            return z

        z = lax.fori_loop(0, HALF // 3, back, tuple(z))
        back_level(0, z)

    def strip_step(t, tn, step):
        a, b = OFF - 4 + step, OFF + 12 - step

        def mine(load):
            return jnp.where(top, load(slice(step, step + 8)), load(slice(8 - step, 16 - step)))

        def put(level, v):
            pltpu.store(tn.at[level, pl.ds(a, 8)], v, mask=top)
            pltpu.store(tn.at[level, pl.ds(b, 8)], v, mask=sub >= 4)

        diff, keep, inv = [mine(lambda r: spar[n, r]) for n in (0, 4, 3)]

        def forward(i, carry):
            for u in range(4):
                level = i * 4 + u
                flat = pl.ds(pl.multiple_of(level * 8, 8), 8)
                around = jnp.where(
                    top,
                    t[level, a - 1:a + 7] + t[level, a + 1:a + 9],
                    t[level, b - 1:b + 7] + t[level, b + 1:b + 9],
                ) + strip_beside[flat]
                e = (keep * tcentre[level] + diff * around) + carry
                te[level] = e
                carry = mine(lambda r: scoef[level, r]) * e
            return carry

        end = lax.fori_loop(0, HALF // 4, forward, mine(lambda r: spar[2, r]))
        z = mine(lambda r: scoef[HALF, r]) * (te[HALF - 1] + swap_ends(end))
        put(HALF - 1, z * inv)

        def back_level(level, z):
            z = mine(lambda r: scoef[level, r]) * (te[level] + z)
            put(level, z * inv)
            return z

        def back(i, z):
            for u in range(3):
                z = back_level(HALF - 2 - (i * 3 + u), z)
            return z

        back_level(0, lax.fori_loop(0, HALF // 3, back, z))

    copies = []
    for step in range(1, STEPS + 1):
        gather(xs[step - 1], step)
        gather_strip(ts[step - 1], step)
        neighbours()
        if step > 1:
            packages(step - 2, step)
        for f in range(2):
            main_field(xs[step - 1], xs[step], f, step)
            if step < STEPS:
                continue
            for c in range(2):
                copies.append(pltpu.make_async_copy(
                    x4.at[f, :, c, pl.ds(OFF, ROWS)], new_state.at[0, f, :, :, pl.ds(128 * c, 128)], sem.at[f, c]
                ))
                copies[-1].start()
        if step < STEPS:
            strip_step(ts[step - 1], ts[step], step)
    gather(xs[STEPS], STEPS)
    packages(STEPS - 1, STEPS)
    for rt in range(2):
        total = zero
        for q in range(NQ):
            value = []
            for c in range(2):
                got = None
                for n in range(STEPS):
                    stale = sub < n + 1 if rt == 0 else sub >= 7 - n
                    at = q * ROWS + 8 * rt
                    v = jnp.tanh(jnp.where(
                        stale,
                        patch[n, q, c, OFF + 8 * rt:OFF + 8 * rt + 8],
                        sums[n, at:at + 8, 128 * c:128 * c + 128],
                    ))
                    got = v if got is None else got + v
                value.append(got * (1.0 / STEPS))
                mean[q, 8 * rt:8 * rt + 8, 128 * c:128 * c + 128] = value[c]
            ring = jnp.where(lane >= 126, value[1], value[0])
            total = jnp.where((lane >= 4 * q) & (lane < 4 * q + 4), roll(ring, 4 * q + 2), total)
        edges[8 * rt:8 * rt + 8] = total
    for copy in copies:
        copy.wait()


def remap_kernel(table, received, west_edges, east_edges, codes, mask, out):
    lane = lanes()
    for rt in range(2):
        rows = slice(8 * rt, 8 * rt + 8)
        west_edge = west_edges[rows]
        east_edge = east_edges[rows]
        picks, first, second, sea = [], [], [], []
        for c in range(2):
            cols = slice(128 * c, 128 * c + 128)
            code = codes[0, rows, cols]
            offset = code & 3
            row = code >> 2
            w = []
            for j in range(2):
                v = jnp.full((8, 128), table[0, 0, j], F32)
                for n in range(1, 4):
                    v = jnp.where(row == n, table[0, n, j], v)
                w.append(v)
            first.append(w[0])
            second.append(w[1])
            picks.append([offset == n for n in range(1, 4)])
            sea.append(mask[0, rows, cols] == 1)
        for q in range(NQ):
            v = [received[q, rows, 128 * c:128 * c + 128] for c in range(2)]
            shifted = [[None] * 5, [None] * 5]
            for c in range(2):
                shifted[c][2] = v[c]
            for d in (1, 2):
                turned = [roll(u, d) for u in v]
                far = roll(west_edge, d - (4 * q + 2))
                shifted[0][2 - d] = jnp.where(lane < d, far, turned[0])
                shifted[1][2 - d] = jnp.where(lane < d, turned[0], turned[1])
                turned = [roll(u, -d) for u in v]
                far = roll(east_edge, 128 - d - (4 * q + 2))
                shifted[0][2 + d] = jnp.where(lane >= 128 - d, turned[1], turned[0])
                shifted[1][2 + d] = jnp.where(lane >= 128 - d, far, turned[1])
            for c in range(2):
                near, beyond = shifted[c][0], shifted[c][1]
                for n in range(1, 4):
                    near = jnp.where(picks[c][n - 1], shifted[c][n], near)
                    beyond = jnp.where(picks[c][n - 1], shifted[c][n + 1], beyond)
                value = first[c] * near + second[c] * beyond
                out[0, q, rows, 128 * c:128 * c + 128] = jnp.where(sea[c], value, 0.0)


def ring(count, step, periodic):
    pairs = [(i, i + step) for i in range(count)]
    if periodic:
        return [(a, b % count) for a, b in pairs]
    return [(a, b) for a, b in pairs if 0 <= b < count]


FRAME = (2, LEV, 2, TALL, 128)
STRIP = (HALF, TALL, 128)


RIMS = (2 * PLANES + STRIPS // 2, HALO, COLS)
HALVES = (2, 2, HALF * ROWS, COLS)


def load(state, params):
    return pl.pallas_call(
        load_kernel,
        out_shape=(pltpu.VMEM(FRAME, F32), jax.ShapeDtypeStruct((STRIPS, ROWS, 128), F32)),
        in_specs=[HBM, HBM],
        out_specs=[VMEM] * 2,
        scratch_shapes=[
            pltpu.VMEM((3, 2, ROWS, COLS), F32),
            pltpu.SemaphoreType.DMA((4, 2, 2)),
            pltpu.SemaphoreType.DMA,
        ],
        compiler_params=params_of(8),
        name="load",
    )(*[pltpu.with_memory_space_constraint(v, pltpu.HBM) for v in (state, params)])


def prepare(x0, params, couple_weight):
    return pl.pallas_call(
        prepare_kernel,
        out_shape=(
            jax.ShapeDtypeStruct(RIMS, F32),
            jax.ShapeDtypeStruct(RIMS, F32),
            pltpu.VMEM((2, 2, 2 * NQ * ROWS, HALF * ROWS), BF16),
            pltpu.VMEM((2, 2, 2 * NQ * 8, HALF * 8), BF16),
            pltpu.VMEM((2, 2, 3 * COLS, COLS), BF16),
            pltpu.VMEM((256, 128), BF16),
            pltpu.VMEM((5, 2, 2, ROWS, 128), F32),
            pltpu.VMEM((2, HALF + 1, 2, ROWS, 128), F32),
            pltpu.VMEM(HALVES, BF16),
            pltpu.VMEM(HALVES, BF16),
        ),
        in_specs=[VMEM] * 3,
        out_specs=[VMEM] * 10,
        compiler_params=params_of(8),
        name="prepare",
    )(x0, params, couple_weight)


def join(strips, west, east, low_rows, high_rows):
    return pl.pallas_call(
        join_kernel,
        out_shape=(
            jax.ShapeDtypeStruct((STRIPS, ROWS, 128), F32),
            jax.ShapeDtypeStruct(RIMS, F32),
            jax.ShapeDtypeStruct(RIMS, F32),
        ),
        in_specs=[VMEM] * 5,
        out_specs=[VMEM] * 3,
        input_output_aliases={3: 1, 4: 2},
        compiler_params=params_of(8),
        name="join",
    )(strips, west, east, low_rows, high_rows)


def inner(strips, x0, xhi, xlo, par, coef, weights, sides, strip_sides):
    flat = HALF * ROWS
    return pl.pallas_call(
        inner_kernel,
        out_shape=(pltpu.VMEM(FRAME, F32), pltpu.VMEM(HALVES, BF16), pltpu.VMEM(HALVES, BF16))
        + (pltpu.VMEM(FRAME, F32),) * 4
        + (pltpu.VMEM(STRIP, F32),) * 4
        + (pltpu.VMEM((STEPS, NQ * ROWS, COLS), F32),),
        in_specs=[VMEM] * 9,
        out_specs=[VMEM] * 12,
        input_output_aliases={1: 0, 2: 1, 3: 2},
        scratch_shapes=[
            pltpu.VMEM((LEV, 2, ROWS, 128), F32),
            pltpu.VMEM((HALF, ROWS, 128), F32),
            pltpu.VMEM((5, ROWS, 128), F32),
            pltpu.VMEM((HALF + 1, ROWS, 128), F32),
            pltpu.VMEM((flat, 256), BF16),
            pltpu.VMEM((2, 2, flat, COLS), F32),
            pltpu.VMEM((flat, 128), F32),
        ],
        compiler_params=params_of(20),
        name="inner",
    )(strips, x0, xhi, xlo, par, coef, weights, sides, strip_sides)


def outer(*args):
    flat = HALF * 8
    return pl.pallas_call(
        outer_kernel,
        out_shape=(
            jax.ShapeDtypeStruct((1, 2, LEV, ROWS, COLS), F32),
            jax.ShapeDtypeStruct((NQ, ROWS, COLS), F32),
            jax.ShapeDtypeStruct((ROWS, 128), F32),
        ) + (pltpu.VMEM(FRAME, F32),) * 5 + (pltpu.VMEM(STRIP, F32),) * 4,
        in_specs=[VMEM] * 17,
        out_specs=[HBM, VMEM, VMEM] + [VMEM] * 9,
        input_output_aliases={8 + n: 3 + n for n in range(9)},
        scratch_shapes=[
            pltpu.VMEM((LEV, 2, 8, 128), F32),
            pltpu.VMEM((HALF, 8, 128), F32),
            pltpu.VMEM((5, 2, 2, 16, 128), F32),
            pltpu.VMEM((2, HALF + 1, 2, 16, 128), F32),
            pltpu.VMEM((5, 16, 128), F32),
            pltpu.VMEM((HALF + 1, 16, 128), F32),
            pltpu.VMEM((2, LEV, 2, 8, 128), F32),
            pltpu.VMEM((2, 2, flat, COLS), BF16),
            pltpu.VMEM((2, 2, flat, COLS), BF16),
            pltpu.VMEM((HALF, 8, 128), F32),
            pltpu.VMEM((flat, 256), BF16),
            pltpu.VMEM((2, 2, flat, COLS), F32),
            pltpu.VMEM((flat, 128), F32),
            pltpu.VMEM((STEPS, NQ, 2, TALL, 128), F32),
            pltpu.SemaphoreType.DMA((2, 2)),
        ],
        compiler_params=params_of(20),
        name="outer",
    )(*args)


def local(state, params, couple_weight, weight_table, intersection_map, sea_mask):
    lon, lat = lax.axis_size("lon"), lax.axis_size("lat")
    x0, strips = load(state, params)
    west = lax.ppermute(strips, "lon", ring(lon, 1, True))
    east = lax.ppermute(strips, "lon", ring(lon, -1, True))
    low_rows, high_rows, weights, narrow, sides, strip_sides, par, coef, xhi, xlo = prepare(
        x0, params, couple_weight
    )
    strips, low_rows, high_rows = join(strips, west, east, low_rows, high_rows)
    below = lax.ppermute(high_rows, "lat", ring(lat, 1, False))
    above = lax.ppermute(low_rows, "lat", ring(lat, -1, False))
    x0, _, _, *frames, sums = inner(strips, x0, xhi, xlo, par, coef, weights, sides, strip_sides)
    new_state, mean, edges, *_ = outer(
        below, above, strips, params, sums, narrow, sides, strip_sides, x0, *frames
    )
    received = lax.ppermute(mean, "comp", [(0, 1), (1, 0)])

    def across(step):
        return [(a * 2 + s, b * 2 + 1 - s) for a, b in ring(lon, step, True) for s in range(2)]

    west_edges = lax.ppermute(edges, ("lon", "comp"), across(1))
    east_edges = lax.ppermute(edges, ("lon", "comp"), across(-1))
    coupled = pl.pallas_call(
        remap_kernel,
        out_shape=jax.ShapeDtypeStruct((1, NQ, ROWS, COLS), F32),
        in_specs=[SMEM] + [VMEM] * 5,
        out_specs=VMEM,
        compiler_params=params_of(16),
        name="remap",
    )(weight_table, received, west_edges, east_edges, intersection_map, sea_mask)
    return new_state, coupled


def solution(mesh):
    placed = (
        P("comp", None, None, "lat", "lon"),
        P("comp", None, None, "lat", "lon"),
        P("comp", None, None, None),
        P("comp", None, None),
        P("comp", "lat", "lon"),
        P("comp", "lat", "lon"),
    )
    return jax.shard_map(
        local,
        mesh=mesh,
        in_specs=placed,
        out_specs=(P("comp", None, None, "lat", "lon"), P("comp", None, "lat", "lon")),
        check_vma=False,
    )
```

profile of v0, /device:TPU:121, one launch (start us, length us, event | category | flops | bytes accessed | tf_op | source)
XLA Modules:
  0.0 59.9 jit_solution(7175936137763276573)
XLA Ops:
  0.6 3.2 %load.1 = (f32[2,64,2,32,128]{4,3,2,1,0:T(8,128)S(1)}, f32[18,16,128]{2,1,0:T(8,128)S(1)}) custom-call(f32[1,2,64,16,256]{4,3,2,1,0:T(8,128)} %state.1, f32[1,3,2,16,256]{4,3,2,1,0:T(8,128)} %params.5), custom_call_target="tpu_custom_call" | custom-call | tf_op jit(solution)/shard_map/load/pallas_call | solution.py:748
  3.9 3.0 %collective-permute-start = (f32[18,16,128]{2,1,0:T(8,128)S(1)}, f32[18,16,128]{2,1,0:T(8,128)S(1)}, u32[]{:S(2)}, u32[]{:S(2)}) collective-permute-start(f32[18,16,128]{2,1,0:T(8,128)S(1)} %get-tuple-element.30.strips), channel_id=1, source_target_pairs={{0,16},{16,32},{32,48},{48,64},{64,80},{80,96},{96,112},{112,128},... | collective-permute-start | bytes 442376 | tf_op jit(solution)/shard_map/ppermute | solution.py:863
  6.9 0.0 collective-permute-start.1
  6.9 0.9 %copy-done = f32[1,3,2,16,256]{4,3,2,1,0:T(8,128)S(1)} copy-done((f32[1,3,2,16,256]{4,3,2,1,0:T(8,128)S(1)}, f32[1,3,2,16,256]{4,3,2,1,0:T(8,128)}, u32[]{:S(2)}) %copy-start) | copy-done | bytes 98328
  7.8 0.7 %copy-done.4 = f32[1,8,2,64]{3,2,1,0:T(2,128)S(1)} copy-done((f32[1,8,2,64]{3,2,1,0:T(2,128)S(1)}, f32[1,8,2,64]{3,2,1,0:T(2,128)}, u32[]{:S(2)}) %copy-start.4) | copy-done | bytes 4120
  8.5 1.2 %prepare.1 = (f32[143,4,256]{2,1,0:T(4,128)S(1)}, f32[143,4,256]{2,1,0:T(4,128)S(1)}, bf16[2,2,256,512]{3,2,1,0:T(8,128)(2,1)S(1)}, bf16[2,2,128,256]{3,2,1,0:T(...) custom-call(f32[2,64,2,32,128]{4,3,2,1,0:T(8,128)S(1)} %get-tuple-el, ...), custom_call_target="tpu_custom_call" | custom-call | tf_op jit(solution)/shard_map/prepare/pallas_call | solution.py:764
  9.7 0.0 collective-permute-done.west
  9.7 5.4 %collective-permute-done.1.east = f32[18,16,128]{2,1,0:T(8,128)S(1)} collective-permute-done((f32[18,16,128]{2,1,0:T(8,128)S(1)}, f32[18,16,128]{2,1,0:T(8,128)S(1)}, u32[]{:S(2)}, u32[]{:S(2)}) %collective-permute-start.1) | collective-permute-done | bytes 147488 | tf_op jit(solution)/shard_map/ppermute | solution.py:864
  15.1 4.8 %collective-permute-start.2 = (f32[143,4,256]{2,1,0:T(4,128)S(1)}, f32[143,4,256]{2,1,0:T(4,128)S(1)}, u32[]{:S(2)}, u32[]{:S(2)}) collective-permute-start(f32[143,4,256]{2,1,0:T(4,128)S(1)} %get-tuple-element.34), channel_id=1, source_target_pairs={{0,2},{2,4},{4,6},{6,8},{8,10},{10,12},{12,14},{1,3},{3,5},{5,7},{... | collective-permute-start | bytes 1757192 | tf_op jit(solution)/shard_map/ppermute | solution.py:869
  19.9 1.9 %collective-permute-start.3 = (f32[143,4,256]{2,1,0:T(4,128)S(1)}, f32[143,4,256]{2,1,0:T(4,128)S(1)}, u32[]{:S(2)}, u32[]{:S(2)}) collective-permute-start(f32[143,4,256]{2,1,0:T(4,128)S(1)} %get-tuple-element.35), channel_id=1, source_target_pairs={{2,0},{4,2},{6,4},{8,6},{10,8},{12,10},{14,12},{3,1},{5,3},{7,5},{... | collective-permute-start | bytes 1757192 | tf_op jit(solution)/shard_map/ppermute | solution.py:870
  21.8 0.0 copy-start.1
  21.8 17.1 %inner.1 = (f32[2,64,2,32,128]{4,3,2,1,0:T(8,128)S(1)}, bf16[2,2,512,256]{3,2,1,0:T(8,128)(2,1)S(1)}, bf16[2,2,512,256]{3,2,1,0:T(8,128)(2,1)S(1)}, f32[2,64,2,3...) custom-call(f32[18,16,128]{2,1,0:T(8,128)S(1)} %get-tuple-element.36, ...), custom_call_target="tpu_custom_call", output_to_operand_aliasing={{0}: (1, {}), {1}: (2, {}), {2}: (3, {})} | custom-call | tf_op jit(solution)/shard_map/inner/pallas_call | solution.py:803
  38.9 0.0 collective-permute-done.2.below
  39.0 0.0 copy-start.5
  39.0 0.0 copy-start.2
  39.0 0.0 copy-start.3
  39.0 12.0 %outer.1 = (f32[1,2,64,16,256]{4,3,2,1,0:T(8,128)}, f32[8,16,256]{2,1,0:T(8,128)S(1)}, f32[16,128]{1,0:T(8,128)S(1)}, f32[2,64,2,32,128]{4,3,2,1,0:T(8,128)S(1)}...) custom-call(f32[143,4,256]{2,1,0:T(4,128)S(1)} %collective-permute-d, ...), custom_call_target="tpu_custom_call", output_to_operand_aliasing={{3}: (8, {}), {4}: (9, {}), {5}: (10, {}), {6}: (11, {}), {... | custom-call | tf_op jit(solution)/shard_map/outer/pallas_call | solution.py:828
  51.0 0.4 collective-permute-start.4
  51.4 0.5 collective-permute-start.5
  52.0 1.2 %collective-permute-start.6 = (f32[16,128]{1,0:T(8,128)S(1)}, f32[16,128]{1,0:T(8,128)S(1)}, u32[]{:S(2)}, u32[]{:S(2)}) collective-permute-start(f32[16,128]{1,0:T(8,128)S(1)} %get-tuple-element.57), channel_id=1, source_target_pairs={{0,241},{1,240},{16,1},{17,0},{32,17},{33,16},{48,33},{49,32},{64,... | collective-permute-start | bytes 24584 | tf_op jit(solution)/shard_map/ppermute | solution.py:881
  53.2 0.1 copy.22.table
  53.3 1.3 %collective-permute-done.5.west_edges = f32[16,128]{1,0:T(8,128)S(1)} collective-permute-done((f32[16,128]{1,0:T(8,128)S(1)}, f32[16,128]{1,0:T(8,128)S(1)}, u32[]{:S(2)}, u32[]{:S(2)}) %collective-permute-start.5) | collective-permute-done | bytes 8224 | tf_op jit(solution)/shard_map/ppermute | solution.py:880
  54.6 3.8 %collective-permute-done.6.east_edges = f32[16,128]{1,0:T(8,128)S(1)} collective-permute-done((f32[16,128]{1,0:T(8,128)S(1)}, f32[16,128]{1,0:T(8,128)S(1)}, u32[]{:S(2)}, u32[]{:S(2)}) %collective-permute-start.6) | collective-permute-done | bytes 8224 | tf_op jit(solution)/shard_map/ppermute | solution.py:881
  58.4 1.5 %remap.1 = f32[1,8,16,256]{3,2,1,0:T(8,128)} custom-call(f32[1,4,2]{2,1,0:T(4,128)S(1)} %copy.22.table, f32[8,16,256]{2,1,0:T(8,128)S(1)} %collective-permute-done.4.received, f32[16,128]{1,0:T(8,128)S(1)} %collective-permute-done.5.west_edges, f32[16,128]{1,0:T(8,128)S(1)} %collective-permute-done.6.east_edges, s32[1,16,256]{2,1,0:T(8,128)S(1)} %copy-done.2, ...), custom_call_target="tpu_custom_call" | custom-call | tf_op jit(solution)/shard_map/remap/pallas_call | solution.py:882
  (9 shorter events, 0.1 us)
Async XLA Ops:
  3.9 5.8 %collective-permute-start = (f32[18,16,128]{2,1,0:T(8,128)S(1)}, f32[18,16,128]{2,1,0:T(8,128)S(1)}, u32[]{:S(2)}, u32[]{:S(2)}) collective-permute-start(f32[18,16,128]{2,1,0:T(8,128)S(1)} %get-tuple-element.30.strips), channel_id=1, source_target_pairs={{0,16},{16,32},{32,48},{48,64},{64,80},{80,96},{96,112},{112,128},... | collective-permute-start | bytes 442376 | tf_op jit(solution)/shard_map/ppermute | solution.py:863
  6.9 8.2 %collective-permute-start.1 = (f32[18,16,128]{2,1,0:T(8,128)S(1)}, f32[18,16,128]{2,1,0:T(8,128)S(1)}, u32[]{:S(2)}, u32[]{:S(2)}) collective-permute-start(f32[18,16,128]{2,1,0:T(8,128)S(1)} %get-tuple-element.30.strips), channel_id=1, source_target_pairs={{0,240},{16,0},{32,16},{48,32},{64,48},{80,64},{96,80},{112,96},{1... | collective-permute-start | bytes 442376 | tf_op jit(solution)/shard_map/ppermute | solution.py:864
  6.9 0.9 %copy-start = (f32[1,3,2,16,256]{4,3,2,1,0:T(8,128)S(1)}, f32[1,3,2,16,256]{4,3,2,1,0:T(8,128)}, u32[]{:S(2)}) copy-start(f32[1,3,2,16,256]{4,3,2,1,0:T(8,128)} %params.5) | copy-start | bytes 294916
  7.8 0.7 %copy-start.4 = (f32[1,8,2,64]{3,2,1,0:T(2,128)S(1)}, f32[1,8,2,64]{3,2,1,0:T(2,128)}, u32[]{:S(2)}) copy-start(f32[1,8,2,64]{3,2,1,0:T(2,128)} %couple_weight.1) | copy-start | bytes 12292
  15.1 23.8 %collective-permute-start.2 = (f32[143,4,256]{2,1,0:T(4,128)S(1)}, f32[143,4,256]{2,1,0:T(4,128)S(1)}, u32[]{:S(2)}, u32[]{:S(2)}) collective-permute-start(f32[143,4,256]{2,1,0:T(4,128)S(1)} %get-tuple-element.34), channel_id=1, source_target_pairs={{0,2},{2,4},{4,6},{6,8},{8,10},{10,12},{12,14},{1,3},{3,5},{5,7},{... | collective-permute-start | bytes 1757192 | tf_op jit(solution)/shard_map/ppermute | solution.py:869
  19.9 19.0 %collective-permute-start.3 = (f32[143,4,256]{2,1,0:T(4,128)S(1)}, f32[143,4,256]{2,1,0:T(4,128)S(1)}, u32[]{:S(2)}, u32[]{:S(2)}) collective-permute-start(f32[143,4,256]{2,1,0:T(4,128)S(1)} %get-tuple-element.35), channel_id=1, source_target_pairs={{2,0},{4,2},{6,4},{8,6},{10,8},{12,10},{14,12},{3,1},{5,3},{7,5},{... | collective-permute-start | bytes 1757192 | tf_op jit(solution)/shard_map/ppermute | solution.py:870
  21.8 17.1 %copy-start.1 = (f32[1,3,2,16,256]{4,3,2,1,0:T(8,128)S(1)}, f32[1,3,2,16,256]{4,3,2,1,0:T(8,128)}, u32[]{:S(2)}) copy-start(f32[1,3,2,16,256]{4,3,2,1,0:T(8,128)} %params.5) | copy-start | bytes 294916
  39.0 14.2 %copy-start.5 = (f32[1,4,2]{1,2,0:T(2,128)S(1)}, f32[1,4,2]{1,2,0:T(2,128)}, u32[]{:S(2)}) copy-start(f32[1,4,2]{1,2,0:T(2,128)} %param.9) | copy-start | bytes 100
  39.0 19.4 %copy-start.2 = (s32[1,16,256]{2,1,0:T(8,128)S(1)}, s32[1,16,256]{2,1,0:T(8,128)}, u32[]{:S(2)}) copy-start(s32[1,16,256]{2,1,0:T(8,128)} %codes.1) | copy-start | bytes 49156
  39.0 19.4 %copy-start.3 = (s32[1,16,256]{2,1,0:T(8,128)S(1)}, s32[1,16,256]{2,1,0:T(8,128)}, u32[]{:S(2)}) copy-start(s32[1,16,256]{2,1,0:T(8,128)} %mask.1) | copy-start | bytes 49156
  51.0 7.3 %collective-permute-start.4 = (f32[8,16,256]{2,1,0:T(8,128)S(1)}, f32[8,16,256]{2,1,0:T(8,128)S(1)}, u32[]{:S(2)}, u32[]{:S(2)}) collective-permute-start(f32[8,16,256]{2,1,0:T(8,128)S(1)} %get-tuple-element.56), channel_id=1, source_target_pairs={{0,1},{1,0},{2,3},{3,2},{4,5},{5,4},{6,7},{7,6},{8,9},{9,8},{10,11... | collective-permute-start | bytes 393224 | tf_op jit(solution)/shard_map/ppermute | solution.py:875
  51.4 3.1 %collective-permute-start.5 = (f32[16,128]{1,0:T(8,128)S(1)}, f32[16,128]{1,0:T(8,128)S(1)}, u32[]{:S(2)}, u32[]{:S(2)}) collective-permute-start(f32[16,128]{1,0:T(8,128)S(1)} %get-tuple-element.57), channel_id=1, source_target_pairs={{0,17},{1,16},{16,33},{17,32},{32,49},{33,48},{48,65},{49,64},{64,... | collective-permute-start | bytes 24584 | tf_op jit(solution)/shard_map/ppermute | solution.py:880
  52.0 6.4 %collective-permute-start.6 = (f32[16,128]{1,0:T(8,128)S(1)}, f32[16,128]{1,0:T(8,128)S(1)}, u32[]{:S(2)}, u32[]{:S(2)}) collective-permute-start(f32[16,128]{1,0:T(8,128)S(1)} %get-tuple-element.57), channel_id=1, source_target_pairs={{0,241},{1,240},{16,1},{17,0},{32,17},{33,16},{48,33},{49,32},{64,... | collective-permute-start | bytes 24584 | tf_op jit(solution)/shard_map/ppermute | solution.py:881
where the time goes:
time: 60.2 us; the launch traced here: 59.9 us
  Pallas kernels  35.1 us (58%)
  starting transfers between devices  11.9 us (20%)
  waiting for transfers between devices  10.5 us (17%)
  local copies, waits for them, and re-layouts  1.71 us (3%)
  between operations  0.75 us (1%)
    pallas_call x1, Pallas kernels, inner(): pl.pallas_call(inner_kernel, out_shape=(pltpu.VMEM(FRAME, F32), pltpu.VME...  17.1 us
    pallas_call x1, Pallas kernels, outer(): pl.pallas_call(outer_kernel, out_shape=(jax.ShapeDtypeStruct((1, 2, LEV,...  12 us
    ppermute x1, waiting for transfers between devices, local(): east = lax.ppermute(strips, 'lon', ring(lon, -1, True))  5.37 us
    ppermute x1, starting transfers between devices, local(): below = lax.ppermute(high_rows, 'lat', ring(lat, 1, False))  4.76 us
    ppermute x1, waiting for transfers between devices, local(): east_edges = lax.ppermute(edges, ('lon', 'comp'), across(-1))  3.79 us
    pallas_call x1, Pallas kernels, load(): pl.pallas_call(load_kernel, out_shape=(pltpu.VMEM(FRAME, F32), jax.ShapeD...  3.23 us
    ppermute x1, starting transfers between devices, local(): west = lax.ppermute(strips, 'lon', ring(lon, 1, True))  3.04 us
    ppermute x1, starting transfers between devices, local(): above = lax.ppermute(low_rows, 'lat', ring(lat, -1, False))  1.92 us
  transfers between devices with their start and end apart: 7, of which 3 were waited for; matrix products, arithmetic and copies ran while one was open for 0% of the time, Pallas kernels for 31%

commit v1 on v0

--- a/solution.py
+++ b/solution.py
@@ -72,16 +72,20 @@
         pair = jnp.where((lane & 8) == 0, first, second)
         return pair if total is None else jnp.where(inside, pair, total)
 
-    def strip(block, carry):
-        for rt in range(2):
-            at = OFF + 8 * rt
-            total = None
-            for lq in range(2):
-                for f in range(2):
-                    for h in range(2):
-                        lam = level_of(block * 2 + lq, h)
-                        source = [x0[f, lam, c, at:at + 8] for c in range(2)]
-                        total = place(total, source, lq * 4 + f * 2 + h)
+    def strip(i, carry):
+        made = []
+        for block in (i * 2, i * 2 + 1):
+            for rt in range(2):
+                at = OFF + 8 * rt
+                total = None
+                for lq in range(2):
+                    for f in range(2):
+                        for h in range(2):
+                            lam = level_of(block * 2 + lq, h)
+                            source = [x0[f, lam, c, at:at + 8] for c in range(2)]
+                            total = place(total, source, lq * 4 + f * 2 + h)
+                made.append((block, rt, total))
+        for block, rt, total in made:
             strips[block, 8 * rt:8 * rt + 8] = total
         return carry
 
@@ -90,7 +94,7 @@
             for f in range(2):
                 for c in range(2):
                     copies[m, f, c].wait()
-        lax.fori_loop(n * part // 2, (n + 1) * part // 2, strip, 0)
+        lax.fori_loop(n * part // 4, (n + 1) * part // 4, strip, 0)
     small.wait()
     for rt in range(2):
         rows = slice(8 * rt, 8 * rt + 8)
@@ -170,20 +174,21 @@
         for n, value in enumerate((h, k, g, 1.0 / k, 1.0 - 4.0 * h)):
             par[n, f, c, rows] = value
 
-    def pivots(level, carry):
+    def pivots(i, carry):
         out = []
         for n, (f, c, rt) in enumerate(columns):
             rows = slice(8 * rt, 8 * rt + 8)
-            k = par[1, f, c, rows]
-            m = k / (1.0 + 2.0 * k - k * carry[n])
-            coef[f, level, c, rows] = m
-            out.append(m)
-        some(level, 0)
+            out.append(pivot_levels(coef, (f,), (c, rows), q[n], carry[n], i * 2, 2))
+        for u in range(2):
+            some(i * 2 + u, 0)
         return tuple(out)
 
-    last = lax.fori_loop(0, HALF, pivots, (jnp.ones((8, 128), F32),) * len(columns))
-    for n, (f, c, rt) in enumerate(columns):
-        coef[f, HALF, c, 8 * rt:8 * rt + 8] = last[n] / (1.0 - last[n] * last[n])
+    q = [ratio(par[1, f, c, 8 * rt:8 * rt + 8]) for f, c, rt in columns]
+    lax.fori_loop(0, HALF // 2, pivots, tuple(q))
+    for f, c, rt in columns:
+        rows = slice(8 * rt, 8 * rt + 8)
+        m = coef[f, HALF - 1, c, rows]
+        coef[f, HALF, c, rows] = m / (1.0 - m * m)
     kron_weights(couple_weight, weights, ROWS)
     kron_weights(couple_weight, narrow, 8)
     row = lax.broadcasted_iota(jnp.int32, (COLS, COLS), 0)
@@ -200,38 +205,51 @@
     near = jnp.abs((row & 127) - col)[:, 0:128] == 1
     strip_sides[...] = near.astype(F32).astype(jnp.bfloat16)
 
+def ratio(k):
+    root = jnp.sqrt(1.0 + 4.0 * k) + 1.0
+    return 4.0 * k / (root * root)
+
+
+def pivot_levels(ref, index, rows, q, power, first, count):
+    square = q * q
+    for u in range(count):
+        above = power * square
+        ref[*index, first + u, *rows] = q * (1.0 + power) / (1.0 + above)
+        power = above
+    return power
+
+
 def strip_params(spar):
     for rt in range(2):
         rows = slice(8 * rt, 8 * rt + 8)
         k = spar[1, rows]
         k = jnp.where(k > 0.0, k, 1.0)
-        spar[1, rows] = k
+        spar[5, rows] = ratio(k)
         spar[3, rows] = 1.0 / k
         spar[4, rows] = 1.0 - 4.0 * spar[0, rows]
 
 
-def strip_pivots(spar, scoef, level, carry):
+def strip_pivots(spar, scoef, first, count, carry):
     out = []
     for rt in range(2):
         rows = slice(8 * rt, 8 * rt + 8)
-        k = spar[1, rows]
-        m = k / (1.0 + 2.0 * k - k * carry[rt])
-        scoef[level, rows] = m
-        out.append(m)
+        out.append(pivot_levels(scoef, (), (rows,), spar[5, rows], carry[rt], first, count))
     return tuple(out)
 
 
-def strip_closing(scoef, last):
+def strip_closing(scoef):
     for rt in range(2):
-        scoef[HALF, 8 * rt:8 * rt + 8] = last[rt] / (1.0 - last[rt] * last[rt])
+        rows = slice(8 * rt, 8 * rt + 8)
+        m = scoef[HALF - 1, rows]
+        scoef[HALF, rows] = m / (1.0 - m * m)
 
 
 def swap_ends(value):
     return jnp.where((lanes() & 16) == 0, roll(value, -16), roll(value, 16))
 
 
-def inner_kernel(strips, x0_in, xhi_in, xlo_in, par, coef, weights, sides, strip_sides,
-                 x0, xhi, xlo, x1, x2, x3, x4, t0, t1, t2, t3, sums,
+def inner_kernel(strips, x0_in, xhi_in, xlo_in, par, coef, weights, narrow, sides, strip_sides,
+                 x0, xhi, xlo, x1, x2, x3, x4, t0, t1, t2, t3, sums, middle,
                  xe, te, spar, scoef, tsplit, beside, strip_beside):
     xs, ts = (x0, x1, x2, x3, x4), (t0, t1, t2, t3)
     sub = subs()
@@ -244,15 +262,18 @@
         spar[2, rows] = strips[HALF // 2 + 1, rows]
     strip_params(spar)
 
-    def unstrip(block, carry):
-        for lq in range(2):
-            level = block * 2 + lq
-            tiles = [roll(strips[block, 8 * rt:8 * rt + 8], 64 * lq) for rt in range(2)]
+    def unstrip(i, carry):
+        levels = []
+        for u in range(4):
+            block = i * 4 + u
+            for lq in range(2):
+                tiles = [roll(strips[block, 8 * rt:8 * rt + 8], 64 * lq) for rt in range(2)]
+                levels.append((block * 2 + lq, tiles))
+        for level, tiles in levels:
             for rt in range(2):
                 t0[level, OFF + 8 * rt:OFF + 8 * rt + 8] = tiles[rt]
             split_strip(level, tiles)
-            carry = strip_pivots(spar, scoef, level, carry)
-        return carry
+        return strip_pivots(spar, scoef, i * 8, 8, carry)
 
     def split_strip(level, tiles):
         at = pl.ds(pl.multiple_of(level * ROWS, 16), ROWS)
@@ -260,8 +281,8 @@
         tsplit[at, 0:128] = high
         tsplit[at, 128:256] = low
 
-    one = jnp.ones((8, 128), F32)
-    strip_closing(scoef, lax.fori_loop(0, HALF // 2, unstrip, (one, one)))
+    lax.fori_loop(0, HALF // 8, unstrip, (spar[5, 0:8], spar[5, 8:16]))
+    strip_closing(scoef)
 
     def vertical(load, rt):
         at = OFF + 8 * rt
@@ -294,15 +315,15 @@
                 total = value if total is None else total + value
         sums[n] = total
 
-    def main_field(x, xn, f):
+    def main_field(x, xn, f, halve):
         tiles = [(c, rt, slice(8 * rt, 8 * rt + 8), OFF + 8 * rt) for c in range(2) for rt in range(2)]
         diff = [par[0, f, c, rows] for c, rt, rows, at in tiles]
         keep = [par[4, f, c, rows] for c, rt, rows, at in tiles]
 
         def forward(i, carry):
             carry = list(carry)
-            for u in range(2):
-                level = i * 2 + u
+            for u in range(4):
+                level = i * 4 + u
                 for n, (c, rt, rows, at) in enumerate(tiles):
                     m = coef[f, level, c, rows]
                     flat = pl.ds(pl.multiple_of(level * ROWS, 8) + 8 * rt, 8)
@@ -316,7 +337,7 @@
             return tuple(carry)
 
         start = tuple(par[2, f, c, rows] for c, rt, rows, at in tiles) + (zero,) * 4
-        ends = lax.fori_loop(0, HALF // 2, forward, start)
+        ends = lax.fori_loop(0, HALF // 4, forward, start)
         inv = [par[3, f, c, rows] for c, rt, rows, at in tiles]
 
         def finish(level, h, z):
@@ -328,6 +349,8 @@
                     v = z[h * 4 + 2 * c + rt] * inv[2 * c + rt]
                     xn[f, lam, c, OFF + 8 * rt:OFF + 8 * rt + 8] = v
                     y.append(v)
+                if not halve:
+                    continue
                 high, low = halves(jnp.concatenate(y, axis=0))
                 xhi[f, h, flat, 128 * c:128 * c + 128] = high
                 xlo[f, h, flat, 128 * c:128 * c + 128] = low
@@ -397,18 +420,109 @@
         z = lax.fori_loop(0, HALF // 3, back, tuple(z))
         back_level(0, z)
 
-    for step in range(STEPS):
+    begin, rows8 = OFF + 4, slice(4, 12)
+
+    def halve_middle(x, t):
+        def some(i, carry):
+            at = pl.ds(pl.multiple_of(i * 16, 16), 16)
+            for f in range(2):
+                for h in range(2):
+                    for c in range(2):
+                        pair = [x[f, level_of(i * 2 + u, h), c, begin:begin + 8] for u in range(2)]
+                        high, low = halves(jnp.concatenate(pair, axis=0))
+                        xhi[f, h, at, 128 * c:128 * c + 128] = high
+                        xlo[f, h, at, 128 * c:128 * c + 128] = low
+            if t is not None:
+                pair = [t[i * 2 + u, begin:begin + 8] for u in range(2)]
+                high, low = halves(jnp.concatenate(pair, axis=0))
+                tsplit[at, 0:128] = high
+                tsplit[at, 128:256] = low
+            return carry
+
+        lax.fori_loop(0, HALF // 2, some, 0)
+
+    def neighbours_middle():
+        for f in range(2):
+            for h in range(2):
+                value = jnp.concatenate([xhi[f, h, 0:256], xlo[f, h, 0:256], tsplit[0:256]], axis=1)
+                beside[f, h, 0:256] = jnp.dot(value, sides[f, h], preferred_element_type=F32)
+
+    def packages_middle(n):
+        total = None
+        for f in range(2):
+            for h in range(2):
+                both = jnp.dot(narrow[f, h], xhi[f, h, 0:256], preferred_element_type=F32)
+                high = jnp.dot(narrow[f, h, :NQ * 8], xlo[f, h, 0:256], preferred_element_type=F32)
+                value = (both[NQ * 8:] + high) + both[:NQ * 8]
+                total = value if total is None else total + value
+        middle[n, 8:8 + NQ * 8] = total
+
+    def main_middle(x, xn, f):
+        diff = [par[0, f, c, rows8] for c in range(2)]
+        keep = [par[4, f, c, rows8] for c in range(2)]
+        inv = [par[3, f, c, rows8] for c in range(2)]
+
+        def forward(i, carry):
+            carry = list(carry)
+            for u in range(8):
+                level = i * 8 + u
+                flat = pl.ds(pl.multiple_of(level * 8, 8), 8)
+                for c in range(2):
+                    m = coef[f, level, c, rows8]
+                    for h in range(2):
+                        lam = level_of(level, h)
+                        around = x[f, lam, c, begin - 1:begin + 7] + x[f, lam, c, begin + 1:begin + 9]
+                        around = around + beside[f, h, flat, 128 * c:128 * c + 128]
+                        e = (keep[c] * x[f, lam, c, begin:begin + 8] + diff[c] * around) + carry[h * 2 + c]
+                        xe[lam, c, 0:8] = e
+                        carry[h * 2 + c] = m * e
+            return tuple(carry)
+
+        start = (par[2, f, 0, rows8], par[2, f, 1, rows8], zero, zero)
+        ends = lax.fori_loop(0, HALF // 8, forward, start)
+        z = []
+        for h in range(2):
+            for c in range(2):
+                v = coef[f, HALF, c, rows8] * (xe[HALF - 1 + h, c, 0:8] + ends[(1 - h) * 2 + c])
+                xn[f, HALF - 1 + h, c, begin:begin + 8] = v * inv[c]
+                z.append(v)
+
+        def back_level(level, z):
+            out = [None] * 4
+            for c in range(2):
+                m = coef[f, level, c, rows8]
+                for h in range(2):
+                    lam = level_of(level, h)
+                    v = m * (xe[lam, c, 0:8] + z[h * 2 + c])
+                    xn[f, lam, c, begin:begin + 8] = v * inv[c]
+                    out[h * 2 + c] = v
+            return tuple(out)
+
+        def back(i, z):
+            for u in range(10):
+                z = back_level(HALF - 2 - (i * 10 + u), z)
+            return z
+
+        z = lax.fori_loop(0, HALF // 10, back, tuple(z))
+        back_level(0, z)
+
+    for step in range(STEPS - 1):
         neighbours()
         if step > 0:
             packages(step - 1)
         for f in range(2):
-            main_field(xs[step], xs[step + 1], f)
-        if step < STEPS - 1:
-            strip_step(ts[step], ts[step + 1])
-    packages(STEPS - 1)
-
-
-def outer_kernel(below, above, strips, params, sums, narrow, sides, strip_sides,
+            main_field(xs[step], xs[step + 1], f, step < STEPS - 2)
+        strip_step(ts[step], ts[step + 1])
+    halve_middle(x3, t3)
+    neighbours_middle()
+    packages_middle(0)
+    for f in range(2):
+        main_middle(x3, x4, f)
+    halve_middle(x4, None)
+    packages_middle(1)
+
+
+def outer_kernel(below, above, strips, params, sums, middle, narrow, sides, strip_sides,
                  i0, i1, i2, i3, i4, j0, j1, j2, j3,
                  new_state, mean, edges, x0, x1, x2, x3, x4, t0, t1, t2, t3,
                  xe, te, par, coef, spar, scoef, centre, xhi, xlo, tcentre, tsplit, beside, strip_beside, patch, sem):
@@ -439,43 +553,42 @@
         rows = slice(8 * rt, 8 * rt + 8)
         k = par[1, f, c, rows]
         k = jnp.where(k > 0.0, k, 1.0)
-        par[1, f, c, rows] = k
+        par[5, f, c, rows] = ratio(k)
         par[3, f, c, rows] = 1.0 / k
         par[4, f, c, rows] = 1.0 - 4.0 * par[0, f, c, rows]
 
-    def pivots(level, carry):
+    def pivots(i, carry):
         out = []
         for n, (f, c, rt) in enumerate(columns):
             rows = slice(8 * rt, 8 * rt + 8)
-            k = par[1, f, c, rows]
-            m = k / (1.0 + 2.0 * k - k * carry[n])
-            coef[f, level, c, rows] = m
-            out.append(m)
-        out.extend(strip_pivots(spar, scoef, level, carry[len(columns):]))
-        for f in range(2):
-            for h in range(2):
-                lam = level_of(level, h)
-                for c in range(2):
-                    cols = slice(128 * c, 128 * c + 128)
-                    x0[f, lam, c, OFF - HALO:OFF] = below[f * PLANES + lam, :, cols]
-                    x0[f, lam, c, OFF + ROWS:OFF + ROWS + HALO] = above[f * PLANES + lam, :, cols]
-        return tuple(out)
-
-    last = lax.fori_loop(0, HALF, pivots, (jnp.ones((8, 128), F32),) * (len(columns) + 2))
-    for n, (f, c, rt) in enumerate(columns):
-        coef[f, HALF, c, 8 * rt:8 * rt + 8] = last[n] / (1.0 - last[n] * last[n])
-    strip_closing(scoef, last[len(columns):])
-
-    def unstrip(i, carry):
+            out.append(pivot_levels(coef, (f,), (c, rows), par[5, f, c, rows], carry[n], i * 4, 4))
+        out.extend(strip_pivots(spar, scoef, i * 4, 4, carry[len(columns):]))
+        for u in range(4):
+            for f in range(2):
+                for h in range(2):
+                    lam = level_of(i * 4 + u, h)
+                    for c in range(2):
+                        cols = slice(128 * c, 128 * c + 128)
+                        x0[f, lam, c, OFF - HALO:OFF] = below[f * PLANES + lam, :, cols]
+                        x0[f, lam, c, OFF + ROWS:OFF + ROWS + HALO] = above[f * PLANES + lam, :, cols]
+        rims = []
         for c in range(2):
             cols = slice(128 * c, 128 * c + 128)
             for lq in range(2):
-                level = i * 4 + c * 2 + lq
-                t0[level, OFF - HALO:OFF] = pltpu.roll(below[2 * PLANES + i, :, cols], 64 * lq, 1)
-                t0[level, OFF + ROWS:OFF + ROWS + HALO] = pltpu.roll(above[2 * PLANES + i, :, cols], 64 * lq, 1)
-        return carry
-
-    lax.fori_loop(0, HALF // 4, unstrip, 0)
+                rims.append(pltpu.roll(below[2 * PLANES + i, :, cols], 64 * lq, 1))
+                rims.append(pltpu.roll(above[2 * PLANES + i, :, cols], 64 * lq, 1))
+        for n in range(4):
+            t0[i * 4 + n, OFF - HALO:OFF] = rims[2 * n]
+            t0[i * 4 + n, OFF + ROWS:OFF + ROWS + HALO] = rims[2 * n + 1]
+        return tuple(out)
+
+    start = [par[5, f, c, 8 * rt:8 * rt + 8] for f, c, rt in columns] + [spar[5, 0:8], spar[5, 8:16]]
+    lax.fori_loop(0, HALF // 4, pivots, tuple(start))
+    for f, c, rt in columns:
+        rows = slice(8 * rt, 8 * rt + 8)
+        m = coef[f, HALF - 1, c, rows]
+        coef[f, HALF, c, rows] = m / (1.0 - m * m)
+    strip_closing(scoef)
 
     def gather(x, step):
         a, b = OFF - 4 + step, OFF + 12 - step
@@ -591,11 +704,11 @@
             return tuple(out)
 
         def back(i, z):
-            for u in range(3):
-                z = back_level(HALF - 2 - (i * 3 + u), z)
+            for u in range(10):
+                z = back_level(HALF - 2 - (i * 10 + u), z)
             return z
 
-        z = lax.fori_loop(0, HALF // 3, back, tuple(z))
+        z = lax.fori_loop(0, HALF // 10, back, tuple(z))
         back_level(0, z)
 
     def strip_step(t, tn, step):
@@ -667,13 +780,14 @@
             for c in range(2):
                 got = None
                 for n in range(STEPS):
-                    stale = sub < n + 1 if rt == 0 else sub >= 7 - n
-                    at = q * ROWS + 8 * rt
-                    v = jnp.tanh(jnp.where(
-                        stale,
-                        patch[n, q, c, OFF + 8 * rt:OFF + 8 * rt + 8],
-                        sums[n, at:at + 8, 128 * c:128 * c + 128],
-                    ))
+                    cols = slice(128 * c, 128 * c + 128)
+                    if n < 2:
+                        stale = sub < n + 1 if rt == 0 else sub >= 7 - n
+                        own = sums[n, q * ROWS + 8 * rt:q * ROWS + 8 * rt + 8, cols]
+                    else:
+                        stale = top if rt == 0 else sub >= 4
+                        own = middle[n - 2, 4 + 8 * q + 8 * rt:12 + 8 * q + 8 * rt, cols]
+                    v = jnp.tanh(jnp.where(stale, patch[n, q, c, OFF + 8 * rt:OFF + 8 * rt + 8], own))
                     got = v if got is None else got + v
                 value.append(got * (1.0 / STEPS))
                 mean[q, 8 * rt:8 * rt + 8, 128 * c:128 * c + 128] = value[c]
@@ -798,21 +912,21 @@
     )(strips, west, east, low_rows, high_rows)
 
 
-def inner(strips, x0, xhi, xlo, par, coef, weights, sides, strip_sides):
+def inner(strips, x0, xhi, xlo, par, coef, weights, narrow, sides, strip_sides):
     flat = HALF * ROWS
     return pl.pallas_call(
         inner_kernel,
         out_shape=(pltpu.VMEM(FRAME, F32), pltpu.VMEM(HALVES, BF16), pltpu.VMEM(HALVES, BF16))
         + (pltpu.VMEM(FRAME, F32),) * 4
         + (pltpu.VMEM(STRIP, F32),) * 4
-        + (pltpu.VMEM((STEPS, NQ * ROWS, COLS), F32),),
-        in_specs=[VMEM] * 9,
-        out_specs=[VMEM] * 12,
+        + (pltpu.VMEM((2, NQ * ROWS, COLS), F32), pltpu.VMEM((2, NQ * 8 + 16, COLS), F32)),
+        in_specs=[VMEM] * 10,
+        out_specs=[VMEM] * 13,
         input_output_aliases={1: 0, 2: 1, 3: 2},
         scratch_shapes=[
             pltpu.VMEM((LEV, 2, ROWS, 128), F32),
             pltpu.VMEM((HALF, ROWS, 128), F32),
-            pltpu.VMEM((5, ROWS, 128), F32),
+            pltpu.VMEM((6, ROWS, 128), F32),
             pltpu.VMEM((HALF + 1, ROWS, 128), F32),
             pltpu.VMEM((flat, 256), BF16),
             pltpu.VMEM((2, 2, flat, COLS), F32),
@@ -820,7 +934,7 @@
         ],
         compiler_params=params_of(20),
         name="inner",
-    )(strips, x0, xhi, xlo, par, coef, weights, sides, strip_sides)
+    )(strips, x0, xhi, xlo, par, coef, weights, narrow, sides, strip_sides)
 
 
 def outer(*args):
@@ -832,15 +946,15 @@
             jax.ShapeDtypeStruct((NQ, ROWS, COLS), F32),
             jax.ShapeDtypeStruct((ROWS, 128), F32),
         ) + (pltpu.VMEM(FRAME, F32),) * 5 + (pltpu.VMEM(STRIP, F32),) * 4,
-        in_specs=[VMEM] * 17,
+        in_specs=[VMEM] * 18,
         out_specs=[HBM, VMEM, VMEM] + [VMEM] * 9,
-        input_output_aliases={8 + n: 3 + n for n in range(9)},
+        input_output_aliases={9 + n: 3 + n for n in range(9)},
         scratch_shapes=[
             pltpu.VMEM((LEV, 2, 8, 128), F32),
             pltpu.VMEM((HALF, 8, 128), F32),
-            pltpu.VMEM((5, 2, 2, 16, 128), F32),
+            pltpu.VMEM((6, 2, 2, 16, 128), F32),
             pltpu.VMEM((2, HALF + 1, 2, 16, 128), F32),
-            pltpu.VMEM((5, 16, 128), F32),
+            pltpu.VMEM((6, 16, 128), F32),
             pltpu.VMEM((HALF + 1, 16, 128), F32),
             pltpu.VMEM((2, LEV, 2, 8, 128), F32),
             pltpu.VMEM((2, 2, flat, COLS), BF16),
@@ -868,9 +982,11 @@
     strips, low_rows, high_rows = join(strips, west, east, low_rows, high_rows)
     below = lax.ppermute(high_rows, "lat", ring(lat, 1, False))
     above = lax.ppermute(low_rows, "lat", ring(lat, -1, False))
-    x0, _, _, *frames, sums = inner(strips, x0, xhi, xlo, par, coef, weights, sides, strip_sides)
+    x0, _, _, *frames, sums, middle = inner(
+        strips, x0, xhi, xlo, par, coef, weights, narrow, sides, strip_sides
+    )
     new_state, mean, edges, *_ = outer(
-        below, above, strips, params, sums, narrow, sides, strip_sides, x0, *frames
+        below, above, strips, params, sums, middle, narrow, sides, strip_sides, x0, *frames
     )
     received = lax.ppermute(mean, "comp", [(0, 1), (1, 0)])
 

time: 60.2 us -> 56 us (0.930)
  Pallas kernels: 35.1 us -> 30.9 us
    pallas_call x1, Pallas kernels: 17.1 us -> 14.2 us  [inner(): pl.pallas_call(inner_kernel, out_shape=(pltpu.VMEM(FRAME, F32), pltpu.VME...]
    pallas_call x1, Pallas kernels: 12 us -> 11.4 us  [outer(): pl.pallas_call(outer_kernel, out_shape=(jax.ShapeDtypeStruct((1, 2, LEV,...]
    unnamed x13 -> x11, local copies, waits for them, and re-layouts: 1.71 us -> 1.7 us
  transfers between devices with their start and end apart: 7 -> 7, of which waited for: 3 -> 3; matrix products, arithmetic and copies ran while one was open for 0% -> 0% of each run, Pallas kernels for 31% -> 28%
where the time goes in v1:
time: 56 us; the launch traced here: 55.7 us
  Pallas kernels  30.9 us (55%)
  starting transfers between devices  11.9 us (21%)
  waiting for transfers between devices  10.5 us (19%)
  local copies, waits for them, and re-layouts  1.7 us (3%)
  between operations  0.74 us (1%)
    pallas_call x1, Pallas kernels, inner(): pl.pallas_call(inner_kernel, out_shape=(pltpu.VMEM(FRAME, F32), pltpu.VME...  14.2 us
    pallas_call x1, Pallas kernels, outer(): pl.pallas_call(outer_kernel, out_shape=(jax.ShapeDtypeStruct((1, 2, LEV,...  11.4 us
    ppermute x1, waiting for transfers between devices, local(): east = lax.ppermute(strips, 'lon', ring(lon, -1, True))  5.4 us
    ppermute x1, starting transfers between devices, local(): below = lax.ppermute(high_rows, 'lat', ring(lat, 1, False))  4.76 us
    ppermute x1, waiting for transfers between devices, local(): east_edges = lax.ppermute(edges, ('lon', 'comp'), across(-1))  3.79 us
    ppermute x1, starting transfers between devices, local(): west = lax.ppermute(strips, 'lon', ring(lon, 1, True))  3.04 us
    pallas_call x1, Pallas kernels, load(): pl.pallas_call(load_kernel, out_shape=(pltpu.VMEM(FRAME, F32), jax.ShapeD...  2.68 us
    ppermute x1, starting transfers between devices, local(): above = lax.ppermute(low_rows, 'lat', ring(lat, -1, False))  1.92 us
  transfers between devices with their start and end apart: 7, of which 3 were waited for; matrix products, arithmetic and copies ran while one was open for 0% of the time, Pallas kernels for 28%

profile of v1, /device:TPU:121, one launch (start us, length us, event | category | flops | bytes accessed | tf_op | source)
XLA Modules:
  0.0 55.7 jit_solution(10747225459873103152)
XLA Ops:
  0.6 2.7 %load.1 = (f32[2,64,2,32,128]{4,3,2,1,0:T(8,128)S(1)}, f32[18,16,128]{2,1,0:T(8,128)S(1)}) custom-call(f32[1,2,64,16,256]{4,3,2,1,0:T(8,128)} %state.1, f32[1,3,2,16,256]{4,3,2,1,0:T(8,128)} %params.5), custom_call_target="tpu_custom_call" | custom-call | tf_op jit(solution)/shard_map/load/pallas_call | solution.py:862
  3.3 3.0 %collective-permute-start = (f32[18,16,128]{2,1,0:T(8,128)S(1)}, f32[18,16,128]{2,1,0:T(8,128)S(1)}, u32[]{:S(2)}, u32[]{:S(2)}) collective-permute-start(f32[18,16,128]{2,1,0:T(8,128)S(1)} %get-tuple-element.31.strips), channel_id=1, source_target_pairs={{0,16},{16,32},{32,48},{48,64},{64,80},{80,96},{96,112},{112,128},... | collective-permute-start | bytes 442376 | tf_op jit(solution)/shard_map/ppermute | solution.py:977
  6.4 0.0 collective-permute-start.1
  6.4 0.9 %copy-done = f32[1,3,2,16,256]{4,3,2,1,0:T(8,128)S(1)} copy-done((f32[1,3,2,16,256]{4,3,2,1,0:T(8,128)S(1)}, f32[1,3,2,16,256]{4,3,2,1,0:T(8,128)}, u32[]{:S(2)}) %copy-start) | copy-done | bytes 98328
  7.3 0.7 %copy-done.3 = f32[1,8,2,64]{3,2,1,0:T(2,128)S(1)} copy-done((f32[1,8,2,64]{3,2,1,0:T(2,128)S(1)}, f32[1,8,2,64]{3,2,1,0:T(2,128)}, u32[]{:S(2)}) %copy-start.3) | copy-done | bytes 4120
  8.0 1.2 %prepare.1 = (f32[143,4,256]{2,1,0:T(4,128)S(1)}, f32[143,4,256]{2,1,0:T(4,128)S(1)}, bf16[2,2,256,512]{3,2,1,0:T(8,128)(2,1)S(1)}, bf16[2,2,128,256]{3,2,1,0:T(...) custom-call(f32[2,64,2,32,128]{4,3,2,1,0:T(8,128)S(1)} %get-tuple-el, ...), custom_call_target="tpu_custom_call" | custom-call | tf_op jit(solution)/shard_map/prepare/pallas_call | solution.py:878
  9.1 5.4 %collective-permute-done.1.east = f32[18,16,128]{2,1,0:T(8,128)S(1)} collective-permute-done((f32[18,16,128]{2,1,0:T(8,128)S(1)}, f32[18,16,128]{2,1,0:T(8,128)S(1)}, u32[]{:S(2)}, u32[]{:S(2)}) %collective-permute-start.1) | collective-permute-done | bytes 147488 | tf_op jit(solution)/shard_map/ppermute | solution.py:978
  14.6 4.8 %collective-permute-start.2 = (f32[143,4,256]{2,1,0:T(4,128)S(1)}, f32[143,4,256]{2,1,0:T(4,128)S(1)}, u32[]{:S(2)}, u32[]{:S(2)}) collective-permute-start(f32[143,4,256]{2,1,0:T(4,128)S(1)} %get-tuple-element.35), channel_id=1, source_target_pairs={{0,2},{2,4},{4,6},{6,8},{8,10},{10,12},{12,14},{1,3},{3,5},{5,7},{... | collective-permute-start | bytes 1757192 | tf_op jit(solution)/shard_map/ppermute | solution.py:983
  19.4 1.9 %collective-permute-start.3 = (f32[143,4,256]{2,1,0:T(4,128)S(1)}, f32[143,4,256]{2,1,0:T(4,128)S(1)}, u32[]{:S(2)}, u32[]{:S(2)}) collective-permute-start(f32[143,4,256]{2,1,0:T(4,128)S(1)} %get-tuple-element.36), channel_id=1, source_target_pairs={{2,0},{4,2},{6,4},{8,6},{10,8},{12,10},{14,12},{3,1},{5,3},{7,5},{... | collective-permute-start | bytes 1757192 | tf_op jit(solution)/shard_map/ppermute | solution.py:984
  21.3 14.2 %inner.1 = (f32[2,64,2,32,128]{4,3,2,1,0:T(8,128)S(1)}, bf16[2,2,512,256]{3,2,1,0:T(8,128)(2,1)S(1)}, bf16[2,2,512,256]{3,2,1,0:T(8,128)(2,1)S(1)}, f32[2,64,2,3...) custom-call(f32[18,16,128]{2,1,0:T(8,128)S(1)} %get-tuple-element.37, ...), custom_call_target="tpu_custom_call", output_to_operand_aliasing={{0}: (1, {}), {1}: (2, {}), {2}: (3, {})} | custom-call | tf_op jit(solution)/shard_map/inner/pallas_call | solution.py:917
  35.5 0.0 collective-permute-done.2.below
  35.5 0.0 collective-permute-done.3.above
  35.5 0.0 copy-start.4
  35.5 0.0 copy-start.1
  35.5 0.0 copy-start.2
  35.5 11.4 %outer.1 = (f32[1,2,64,16,256]{4,3,2,1,0:T(8,128)}, f32[8,16,256]{2,1,0:T(8,128)S(1)}, f32[16,128]{1,0:T(8,128)S(1)}, f32[2,64,2,32,128]{4,3,2,1,0:T(8,128)S(1)}...) custom-call(f32[143,4,256]{2,1,0:T(4,128)S(1)} %collective-permute-d, ...), custom_call_target="tpu_custom_call", output_to_operand_aliasing={{3}: (9, {}), {4}: (10, {}), {5}: (11, {}), {6}: (12, {}), ... | custom-call | tf_op jit(solution)/shard_map/outer/pallas_call | solution.py:942
  46.9 0.4 collective-permute-start.4
  47.3 0.5 collective-permute-start.5
  47.8 1.2 %collective-permute-start.6 = (f32[16,128]{1,0:T(8,128)S(1)}, f32[16,128]{1,0:T(8,128)S(1)}, u32[]{:S(2)}, u32[]{:S(2)}) collective-permute-start(f32[16,128]{1,0:T(8,128)S(1)} %get-tuple-element.59), channel_id=1, source_target_pairs={{0,241},{1,240},{16,1},{17,0},{32,17},{33,16},{48,33},{49,32},{64,... | collective-permute-start | bytes 24584 | tf_op jit(solution)/shard_map/ppermute | solution.py:997
  49.0 0.1 copy.22.table
  49.1 1.3 %collective-permute-done.5.west_edges = f32[16,128]{1,0:T(8,128)S(1)} collective-permute-done((f32[16,128]{1,0:T(8,128)S(1)}, f32[16,128]{1,0:T(8,128)S(1)}, u32[]{:S(2)}, u32[]{:S(2)}) %collective-permute-start.5) | collective-permute-done | bytes 8224 | tf_op jit(solution)/shard_map/ppermute | solution.py:996
  50.4 3.8 %collective-permute-done.6.east_edges = f32[16,128]{1,0:T(8,128)S(1)} collective-permute-done((f32[16,128]{1,0:T(8,128)S(1)}, f32[16,128]{1,0:T(8,128)S(1)}, u32[]{:S(2)}, u32[]{:S(2)}) %collective-permute-start.6) | collective-permute-done | bytes 8224 | tf_op jit(solution)/shard_map/ppermute | solution.py:997
  54.2 0.0 collective-permute-done.4.received
  54.2 1.5 %remap.1 = f32[1,8,16,256]{3,2,1,0:T(8,128)} custom-call(f32[1,4,2]{2,1,0:T(4,128)S(1)} %copy.22.table, f32[8,16,256]{2,1,0:T(8,128)S(1)} %collective-permute-done.4.received, f32[16,128]{1,0:T(8,128)S(1)} %collective-permute-done.5.west_edges, f32[16,128]{1,0:T(8,128)S(1)} %collective-permute-done.6.east_edges, s32[1,16,256]{2,1,0:T(8,128)S(1)} %copy-done.1, ...), custom_call_target="tpu_custom_call" | custom-call | tf_op jit(solution)/shard_map/remap/pallas_call | solution.py:998
  (7 shorter events, 0.1 us)
Async XLA Ops:
  3.3 5.8 %collective-permute-start = (f32[18,16,128]{2,1,0:T(8,128)S(1)}, f32[18,16,128]{2,1,0:T(8,128)S(1)}, u32[]{:S(2)}, u32[]{:S(2)}) collective-permute-start(f32[18,16,128]{2,1,0:T(8,128)S(1)} %get-tuple-element.31.strips), channel_id=1, source_target_pairs={{0,16},{16,32},{32,48},{48,64},{64,80},{80,96},{96,112},{112,128},... | collective-permute-start | bytes 442376 | tf_op jit(solution)/shard_map/ppermute | solution.py:977
  6.4 8.2 %collective-permute-start.1 = (f32[18,16,128]{2,1,0:T(8,128)S(1)}, f32[18,16,128]{2,1,0:T(8,128)S(1)}, u32[]{:S(2)}, u32[]{:S(2)}) collective-permute-start(f32[18,16,128]{2,1,0:T(8,128)S(1)} %get-tuple-element.31.strips), channel_id=1, source_target_pairs={{0,240},{16,0},{32,16},{48,32},{64,48},{80,64},{96,80},{112,96},{1... | collective-permute-start | bytes 442376 | tf_op jit(solution)/shard_map/ppermute | solution.py:978
  6.4 0.9 %copy-start = (f32[1,3,2,16,256]{4,3,2,1,0:T(8,128)S(1)}, f32[1,3,2,16,256]{4,3,2,1,0:T(8,128)}, u32[]{:S(2)}) copy-start(f32[1,3,2,16,256]{4,3,2,1,0:T(8,128)} %params.5) | copy-start | bytes 294916
  7.3 0.7 %copy-start.3 = (f32[1,8,2,64]{3,2,1,0:T(2,128)S(1)}, f32[1,8,2,64]{3,2,1,0:T(2,128)}, u32[]{:S(2)}) copy-start(f32[1,8,2,64]{3,2,1,0:T(2,128)} %couple_weight.1) | copy-start | bytes 12292
  14.6 20.9 %collective-permute-start.2 = (f32[143,4,256]{2,1,0:T(4,128)S(1)}, f32[143,4,256]{2,1,0:T(4,128)S(1)}, u32[]{:S(2)}, u32[]{:S(2)}) collective-permute-start(f32[143,4,256]{2,1,0:T(4,128)S(1)} %get-tuple-element.35), channel_id=1, source_target_pairs={{0,2},{2,4},{4,6},{6,8},{8,10},{10,12},{12,14},{1,3},{3,5},{5,7},{... | collective-permute-start | bytes 1757192 | tf_op jit(solution)/shard_map/ppermute | solution.py:983
  19.4 16.1 %collective-permute-start.3 = (f32[143,4,256]{2,1,0:T(4,128)S(1)}, f32[143,4,256]{2,1,0:T(4,128)S(1)}, u32[]{:S(2)}, u32[]{:S(2)}) collective-permute-start(f32[143,4,256]{2,1,0:T(4,128)S(1)} %get-tuple-element.36), channel_id=1, source_target_pairs={{2,0},{4,2},{6,4},{8,6},{10,8},{12,10},{14,12},{3,1},{5,3},{7,5},{... | collective-permute-start | bytes 1757192 | tf_op jit(solution)/shard_map/ppermute | solution.py:984
  35.5 13.5 %copy-start.4 = (f32[1,4,2]{1,2,0:T(2,128)S(1)}, f32[1,4,2]{1,2,0:T(2,128)}, u32[]{:S(2)}) copy-start(f32[1,4,2]{1,2,0:T(2,128)} %param.9) | copy-start | bytes 100
  35.5 18.7 %copy-start.1 = (s32[1,16,256]{2,1,0:T(8,128)S(1)}, s32[1,16,256]{2,1,0:T(8,128)}, u32[]{:S(2)}) copy-start(s32[1,16,256]{2,1,0:T(8,128)} %codes.1) | copy-start | bytes 49156
  35.5 18.7 %copy-start.2 = (s32[1,16,256]{2,1,0:T(8,128)S(1)}, s32[1,16,256]{2,1,0:T(8,128)}, u32[]{:S(2)}) copy-start(s32[1,16,256]{2,1,0:T(8,128)} %mask.1) | copy-start | bytes 49156
  46.9 7.3 %collective-permute-start.4 = (f32[8,16,256]{2,1,0:T(8,128)S(1)}, f32[8,16,256]{2,1,0:T(8,128)S(1)}, u32[]{:S(2)}, u32[]{:S(2)}) collective-permute-start(f32[8,16,256]{2,1,0:T(8,128)S(1)} %get-tuple-element.58), channel_id=1, source_target_pairs={{0,1},{1,0},{2,3},{3,2},{4,5},{5,4},{6,7},{7,6},{8,9},{9,8},{10,11... | collective-permute-start | bytes 393224 | tf_op jit(solution)/shard_map/ppermute | solution.py:991
  47.3 3.1 %collective-permute-start.5 = (f32[16,128]{1,0:T(8,128)S(1)}, f32[16,128]{1,0:T(8,128)S(1)}, u32[]{:S(2)}, u32[]{:S(2)}) collective-permute-start(f32[16,128]{1,0:T(8,128)S(1)} %get-tuple-element.59), channel_id=1, source_target_pairs={{0,17},{1,16},{16,33},{17,32},{32,49},{33,48},{48,65},{49,64},{64,... | collective-permute-start | bytes 24584 | tf_op jit(solution)/shard_map/ppermute | solution.py:996
  47.8 6.4 %collective-permute-start.6 = (f32[16,128]{1,0:T(8,128)S(1)}, f32[16,128]{1,0:T(8,128)S(1)}, u32[]{:S(2)}, u32[]{:S(2)}) collective-permute-start(f32[16,128]{1,0:T(8,128)S(1)} %get-tuple-element.59), channel_id=1, source_target_pairs={{0,241},{1,240},{16,1},{17,0},{32,17},{33,16},{48,33},{49,32},{64,... | collective-permute-start | bytes 24584 | tf_op jit(solution)/shard_map/ppermute | solution.py:997

commit v2 on v1

--- a/solution.py
+++ b/solution.py
@@ -387,8 +387,8 @@
 
         def forward(i, carry):
             carry = list(carry)
-            for u in range(4):
-                level = i * 4 + u
+            for u in range(8):
+                level = i * 8 + u
                 for rt, rows in enumerate(tiles):
                     flat = pl.ds(pl.multiple_of(level * ROWS, 8) + 8 * rt, 8)
                     around = vertical(lambda r: t[level, r:r + 8], rt) + strip_beside[flat]
@@ -397,7 +397,7 @@
                     carry[rt] = scoef[level, rows] * e
             return tuple(carry)
 
-        ends = lax.fori_loop(0, HALF // 4, forward, tuple(spar[2, rows] for rows in tiles))
+        ends = lax.fori_loop(0, HALF // 8, forward, tuple(spar[2, rows] for rows in tiles))
         def finish(level, z):
             y = [z[rt] * inv[rt] for rt in range(2)]
             for rt in range(2):
@@ -413,11 +413,11 @@
             return tuple(out)
 
         def back(i, z):
-            for u in range(3):
-                z = back_level(HALF - 2 - (i * 3 + u), z)
+            for u in range(10):
+                z = back_level(HALF - 2 - (i * 10 + u), z)
             return z
 
-        z = lax.fori_loop(0, HALF // 3, back, tuple(z))
+        z = lax.fori_loop(0, HALF // 10, back, tuple(z))
         back_level(0, z)
 
     begin, rows8 = OFF + 4, slice(4, 12)
@@ -530,25 +530,31 @@
     lane, sub = lanes(), subs()
     top = sub < 4
     zero = jnp.zeros((8, 128), F32)
-
-    def strip_rim(ref, block):
-        return ref[2 * PLANES + block // 2, :, 128 * (block % 2):128 * (block % 2) + 128]
+    here = lax.axis_index("lat")
+    outside = [jnp.full((HALO, 128), here, jnp.int32) == end for end in (0, lax.axis_size("lat") - 1)]
+
+    def rim(n, plane, c):
+        ref = (below, above)[n]
+        return jnp.where(outside[n], 0.0, ref[plane, :, 128 * c:128 * c + 128])
+
+    def strip_rim(n, block):
+        return rim(n, 2 * PLANES + block // 2, block % 2)
 
     for n, (block, shift) in enumerate(((HALF // 2, 0), (HALF // 2, 64), (HALF // 2 + 1, 0))):
-        spar[n, 0:4] = pltpu.roll(strip_rim(below, block), shift, 1)
+        spar[n, 0:4] = pltpu.roll(strip_rim(0, block), shift, 1)
         spar[n, 4:8] = pltpu.roll(strips[block, 0:4], shift, 1)
         spar[n, 8:12] = pltpu.roll(strips[block, 12:16], shift, 1)
-        spar[n, 12:16] = pltpu.roll(strip_rim(above, block), shift, 1)
+        spar[n, 12:16] = pltpu.roll(strip_rim(1, block), shift, 1)
     strip_params(spar)
     columns = [(f, c, rt) for f in range(2) for c in range(2) for rt in range(2)]
     for f in range(2):
         for c in range(2):
             cols = slice(128 * c, 128 * c + 128)
             for n in range(3):
-                par[n, f, c, 0:4] = below[f * PLANES + LEV + n, :, cols]
+                par[n, f, c, 0:4] = rim(0, f * PLANES + LEV + n, c)
                 par[n, f, c, 4:8] = params[0, n, f, 0:4, cols]
                 par[n, f, c, 8:12] = params[0, n, f, 12:16, cols]
-                par[n, f, c, 12:16] = above[f * PLANES + LEV + n, :, cols]
+                par[n, f, c, 12:16] = rim(1, f * PLANES + LEV + n, c)
     for f, c, rt in columns:
         rows = slice(8 * rt, 8 * rt + 8)
         k = par[1, f, c, rows]
@@ -568,15 +574,13 @@
                 for h in range(2):
                     lam = level_of(i * 4 + u, h)
                     for c in range(2):
-                        cols = slice(128 * c, 128 * c + 128)
-                        x0[f, lam, c, OFF - HALO:OFF] = below[f * PLANES + lam, :, cols]
-                        x0[f, lam, c, OFF + ROWS:OFF + ROWS + HALO] = above[f * PLANES + lam, :, cols]
+                        x0[f, lam, c, OFF - HALO:OFF] = rim(0, f * PLANES + lam, c)
+                        x0[f, lam, c, OFF + ROWS:OFF + ROWS + HALO] = rim(1, f * PLANES + lam, c)
         rims = []
         for c in range(2):
-            cols = slice(128 * c, 128 * c + 128)
             for lq in range(2):
-                rims.append(pltpu.roll(below[2 * PLANES + i, :, cols], 64 * lq, 1))
-                rims.append(pltpu.roll(above[2 * PLANES + i, :, cols], 64 * lq, 1))
+                for n in range(2):
+                    rims.append(pltpu.roll(rim(n, 2 * PLANES + i, c), 64 * lq, 1))
         for n in range(4):
             t0[i * 4 + n, OFF - HALO:OFF] = rims[2 * n]
             t0[i * 4 + n, OFF + ROWS:OFF + ROWS + HALO] = rims[2 * n + 1]
@@ -724,8 +728,8 @@
         diff, keep, inv = [mine(lambda r: spar[n, r]) for n in (0, 4, 3)]
 
         def forward(i, carry):
-            for u in range(4):
-                level = i * 4 + u
+            for u in range(16):
+                level = i * 16 + u
                 flat = pl.ds(pl.multiple_of(level * 8, 8), 8)
                 around = jnp.where(
                     top,
@@ -737,7 +741,7 @@
                 carry = mine(lambda r: scoef[level, r]) * e
             return carry
 
-        end = lax.fori_loop(0, HALF // 4, forward, mine(lambda r: spar[2, r]))
+        end = lax.fori_loop(0, HALF // 16, forward, mine(lambda r: spar[2, r]))
         z = mine(lambda r: scoef[HALF, r]) * (te[HALF - 1] + swap_ends(end))
         put(HALF - 1, z * inv)
 
@@ -747,11 +751,11 @@
             return z
 
         def back(i, z):
-            for u in range(3):
-                z = back_level(HALF - 2 - (i * 3 + u), z)
+            for u in range(10):
+                z = back_level(HALF - 2 - (i * 10 + u), z)
             return z
 
-        back_level(0, lax.fori_loop(0, HALF // 3, back, z))
+        back_level(0, lax.fori_loop(0, HALF // 10, back, z))
 
     copies = []
     for step in range(1, STEPS + 1):
@@ -980,8 +984,8 @@
         x0, params, couple_weight
     )
     strips, low_rows, high_rows = join(strips, west, east, low_rows, high_rows)
-    below = lax.ppermute(high_rows, "lat", ring(lat, 1, False))
-    above = lax.ppermute(low_rows, "lat", ring(lat, -1, False))
+    below = lax.ppermute(high_rows, "lat", ring(lat, 1, True))
+    above = lax.ppermute(low_rows, "lat", ring(lat, -1, True))
     x0, _, _, *frames, sums, middle = inner(
         strips, x0, xhi, xlo, par, coef, weights, narrow, sides, strip_sides
     )

time: 56 us -> 54.4 us (0.971)
  the two profiles are of different devices: /device:TPU:121 before, /device:TPU:25 now
where the time goes in v2:
time: 54.4 us; the launch traced here: 54.2 us
  Pallas kernels  30.2 us (56%)
  starting transfers between devices  11.1 us (20%)
  waiting for transfers between devices  10.5 us (19%)
  local copies, waits for them, and re-layouts  1.7 us (3%)
  between operations  0.72 us (1%)
    pallas_call x1, Pallas kernels, inner(): pl.pallas_call(inner_kernel, out_shape=(pltpu.VMEM(FRAME, F32), pltpu.VME...  13.9 us
    pallas_call x1, Pallas kernels, outer(): pl.pallas_call(outer_kernel, out_shape=(jax.ShapeDtypeStruct((1, 2, LEV,...  10.9 us
    ppermute x1, waiting for transfers between devices, local(): east = lax.ppermute(strips, 'lon', ring(lon, -1, True))  5.4 us
    ppermute x1, starting transfers between devices, local(): above = lax.ppermute(low_rows, 'lat', ring(lat, -1, True))  4.21 us
    ppermute x1, waiting for transfers between devices, local(): east_edges = lax.ppermute(edges, ('lon', 'comp'), across(-1))  3.78 us
    ppermute x1, starting transfers between devices, local(): west = lax.ppermute(strips, 'lon', ring(lon, 1, True))  3.04 us
    pallas_call x1, Pallas kernels, load(): pl.pallas_call(load_kernel, out_shape=(pltpu.VMEM(FRAME, F32), jax.ShapeD...  2.68 us
    ppermute x1, starting transfers between devices, local(): below = lax.ppermute(high_rows, 'lat', ring(lat, 1, True))  1.71 us
  transfers between devices with their start and end apart: 7, of which 3 were waited for; matrix products, arithmetic and copies ran while one was open for 0% of the time, Pallas kernels for 28%

profile of v2, /device:TPU:25, one launch (start us, length us, event | category | flops | bytes accessed | tf_op | source)
XLA Modules:
  0.0 54.2 jit_solution(8317202813534378685)
XLA Ops:
  0.6 2.7 %load.1 = (f32[2,64,2,32,128]{4,3,2,1,0:T(8,128)S(1)}, f32[18,16,128]{2,1,0:T(8,128)S(1)}) custom-call(f32[1,2,64,16,256]{4,3,2,1,0:T(8,128)} %state.1, f32[1,3,2,16,256]{4,3,2,1,0:T(8,128)} %params.5), custom_call_target="tpu_custom_call" | custom-call | tf_op jit(solution)/shard_map/load/pallas_call | solution.py:866
  3.3 3.0 %collective-permute-start = (f32[18,16,128]{2,1,0:T(8,128)S(1)}, f32[18,16,128]{2,1,0:T(8,128)S(1)}, u32[]{:S(2)}, u32[]{:S(2)}) collective-permute-start(f32[18,16,128]{2,1,0:T(8,128)S(1)} %get-tuple-element.31.strips), channel_id=1, source_target_pairs={{0,16},{16,32},{32,48},{48,64},{64,80},{80,96},{96,112},{112,128},... | collective-permute-start | bytes 442376 | tf_op jit(solution)/shard_map/ppermute | solution.py:981
  6.4 0.0 collective-permute-start.1
  6.4 0.9 %copy-done = f32[1,3,2,16,256]{4,3,2,1,0:T(8,128)S(1)} copy-done((f32[1,3,2,16,256]{4,3,2,1,0:T(8,128)S(1)}, f32[1,3,2,16,256]{4,3,2,1,0:T(8,128)}, u32[]{:S(2)}) %copy-start) | copy-done | bytes 98328
  7.3 0.7 %copy-done.3 = f32[1,8,2,64]{3,2,1,0:T(2,128)S(1)} copy-done((f32[1,8,2,64]{3,2,1,0:T(2,128)S(1)}, f32[1,8,2,64]{3,2,1,0:T(2,128)}, u32[]{:S(2)}) %copy-start.3) | copy-done | bytes 4120
  8.0 1.2 %prepare.1 = (f32[143,4,256]{2,1,0:T(4,128)S(1)}, f32[143,4,256]{2,1,0:T(4,128)S(1)}, bf16[2,2,256,512]{3,2,1,0:T(8,128)(2,1)S(1)}, bf16[2,2,128,256]{3,2,1,0:T(...) custom-call(f32[2,64,2,32,128]{4,3,2,1,0:T(8,128)S(1)} %get-tuple-el, ...), custom_call_target="tpu_custom_call" | custom-call | tf_op jit(solution)/shard_map/prepare/pallas_call | solution.py:882
  9.1 0.0 collective-permute-done.west
  9.1 5.4 %collective-permute-done.1.east = f32[18,16,128]{2,1,0:T(8,128)S(1)} collective-permute-done((f32[18,16,128]{2,1,0:T(8,128)S(1)}, f32[18,16,128]{2,1,0:T(8,128)S(1)}, u32[]{:S(2)}, u32[]{:S(2)}) %collective-permute-start.1) | collective-permute-done | bytes 147488 | tf_op jit(solution)/shard_map/ppermute | solution.py:982
  14.6 1.7 %collective-permute-start.2 = (f32[143,4,256]{2,1,0:T(4,128)S(1)}, f32[143,4,256]{2,1,0:T(4,128)S(1)}, u32[]{:S(2)}, u32[]{:S(2)}) collective-permute-start(f32[143,4,256]{2,1,0:T(4,128)S(1)} %get-tuple-element.35), channel_id=1, source_target_pairs={{0,2},{2,4},{4,6},{6,8},{8,10},{10,12},{12,14},{14,0},{1,3},{3,5},... | collective-permute-start | bytes 1757192 | tf_op jit(solution)/shard_map/ppermute | solution.py:987
  16.3 4.2 %collective-permute-start.3 = (f32[143,4,256]{2,1,0:T(4,128)S(1)}, f32[143,4,256]{2,1,0:T(4,128)S(1)}, u32[]{:S(2)}, u32[]{:S(2)}) collective-permute-start(f32[143,4,256]{2,1,0:T(4,128)S(1)} %get-tuple-element.36), channel_id=1, source_target_pairs={{0,14},{2,0},{4,2},{6,4},{8,6},{10,8},{12,10},{14,12},{1,15},{3,1}... | collective-permute-start | bytes 1757192 | tf_op jit(solution)/shard_map/ppermute | solution.py:988
  20.5 13.9 %inner.1 = (f32[2,64,2,32,128]{4,3,2,1,0:T(8,128)S(1)}, bf16[2,2,512,256]{3,2,1,0:T(8,128)(2,1)S(1)}, bf16[2,2,512,256]{3,2,1,0:T(8,128)(2,1)S(1)}, f32[2,64,2,3...) custom-call(f32[18,16,128]{2,1,0:T(8,128)S(1)} %get-tuple-element.37, ...), custom_call_target="tpu_custom_call", output_to_operand_aliasing={{0}: (1, {}), {1}: (2, {}), {2}: (3, {})} | custom-call | tf_op jit(solution)/shard_map/inner/pallas_call | solution.py:921
  34.4 0.0 collective-permute-done.2.below
  34.4 0.0 copy-start.4
  34.4 0.0 copy-start.1
  34.4 0.0 copy-start.2
  34.4 10.9 %outer.1 = (f32[1,2,64,16,256]{4,3,2,1,0:T(8,128)}, f32[8,16,256]{2,1,0:T(8,128)S(1)}, f32[16,128]{1,0:T(8,128)S(1)}, f32[2,64,2,32,128]{4,3,2,1,0:T(8,128)S(1)}...) custom-call(f32[143,4,256]{2,1,0:T(4,128)S(1)} %collective-permute-d, ...), custom_call_target="tpu_custom_call", output_to_operand_aliasing={{3}: (9, {}), {4}: (10, {}), {5}: (11, {}), {6}: (12, {}), ... | custom-call | tf_op jit(solution)/shard_map/outer/pallas_call | solution.py:946
  45.4 0.4 collective-permute-start.4
  45.8 0.5 collective-permute-start.5
  46.3 1.2 %collective-permute-start.6 = (f32[16,128]{1,0:T(8,128)S(1)}, f32[16,128]{1,0:T(8,128)S(1)}, u32[]{:S(2)}, u32[]{:S(2)}) collective-permute-start(f32[16,128]{1,0:T(8,128)S(1)} %get-tuple-element.59), channel_id=1, source_target_pairs={{0,241},{1,240},{16,1},{17,0},{32,17},{33,16},{48,33},{49,32},{64,... | collective-permute-start | bytes 24584 | tf_op jit(solution)/shard_map/ppermute | solution.py:1001
  47.5 0.1 copy.22.table
  47.6 1.3 %collective-permute-done.5.west_edges = f32[16,128]{1,0:T(8,128)S(1)} collective-permute-done((f32[16,128]{1,0:T(8,128)S(1)}, f32[16,128]{1,0:T(8,128)S(1)}, u32[]{:S(2)}, u32[]{:S(2)}) %collective-permute-start.5) | collective-permute-done | bytes 8224 | tf_op jit(solution)/shard_map/ppermute | solution.py:1000
  48.9 3.8 %collective-permute-done.6.east_edges = f32[16,128]{1,0:T(8,128)S(1)} collective-permute-done((f32[16,128]{1,0:T(8,128)S(1)}, f32[16,128]{1,0:T(8,128)S(1)}, u32[]{:S(2)}, u32[]{:S(2)}) %collective-permute-start.6) | collective-permute-done | bytes 8224 | tf_op jit(solution)/shard_map/ppermute | solution.py:1001
  52.7 0.0 collective-permute-done.4.received
  52.7 1.5 %remap.1 = f32[1,8,16,256]{3,2,1,0:T(8,128)} custom-call(f32[1,4,2]{2,1,0:T(4,128)S(1)} %copy.22.table, f32[8,16,256]{2,1,0:T(8,128)S(1)} %collective-permute-done.4.received, f32[16,128]{1,0:T(8,128)S(1)} %collective-permute-done.5.west_edges, f32[16,128]{1,0:T(8,128)S(1)} %collective-permute-done.6.east_edges, s32[1,16,256]{2,1,0:T(8,128)S(1)} %copy-done.1, ...), custom_call_target="tpu_custom_call" | custom-call | tf_op jit(solution)/shard_map/remap/pallas_call | solution.py:1002
  (7 shorter events, 0.1 us)
Async XLA Ops:
  3.3 5.8 %collective-permute-start = (f32[18,16,128]{2,1,0:T(8,128)S(1)}, f32[18,16,128]{2,1,0:T(8,128)S(1)}, u32[]{:S(2)}, u32[]{:S(2)}) collective-permute-start(f32[18,16,128]{2,1,0:T(8,128)S(1)} %get-tuple-element.31.strips), channel_id=1, source_target_pairs={{0,16},{16,32},{32,48},{48,64},{64,80},{80,96},{96,112},{112,128},... | collective-permute-start | bytes 442376 | tf_op jit(solution)/shard_map/ppermute | solution.py:981
  6.4 8.2 %collective-permute-start.1 = (f32[18,16,128]{2,1,0:T(8,128)S(1)}, f32[18,16,128]{2,1,0:T(8,128)S(1)}, u32[]{:S(2)}, u32[]{:S(2)}) collective-permute-start(f32[18,16,128]{2,1,0:T(8,128)S(1)} %get-tuple-element.31.strips), channel_id=1, source_target_pairs={{0,240},{16,0},{32,16},{48,32},{64,48},{80,64},{96,80},{112,96},{1... | collective-permute-start | bytes 442376 | tf_op jit(solution)/shard_map/ppermute | solution.py:982
  6.4 0.9 %copy-start = (f32[1,3,2,16,256]{4,3,2,1,0:T(8,128)S(1)}, f32[1,3,2,16,256]{4,3,2,1,0:T(8,128)}, u32[]{:S(2)}) copy-start(f32[1,3,2,16,256]{4,3,2,1,0:T(8,128)} %params.5) | copy-start | bytes 294916
  7.3 0.7 %copy-start.3 = (f32[1,8,2,64]{3,2,1,0:T(2,128)S(1)}, f32[1,8,2,64]{3,2,1,0:T(2,128)}, u32[]{:S(2)}) copy-start(f32[1,8,2,64]{3,2,1,0:T(2,128)} %couple_weight.1) | copy-start | bytes 12292
  14.6 19.8 %collective-permute-start.2 = (f32[143,4,256]{2,1,0:T(4,128)S(1)}, f32[143,4,256]{2,1,0:T(4,128)S(1)}, u32[]{:S(2)}, u32[]{:S(2)}) collective-permute-start(f32[143,4,256]{2,1,0:T(4,128)S(1)} %get-tuple-element.35), channel_id=1, source_target_pairs={{0,2},{2,4},{4,6},{6,8},{8,10},{10,12},{12,14},{14,0},{1,3},{3,5},... | collective-permute-start | bytes 1757192 | tf_op jit(solution)/shard_map/ppermute | solution.py:987
  16.3 18.1 %collective-permute-start.3 = (f32[143,4,256]{2,1,0:T(4,128)S(1)}, f32[143,4,256]{2,1,0:T(4,128)S(1)}, u32[]{:S(2)}, u32[]{:S(2)}) collective-permute-start(f32[143,4,256]{2,1,0:T(4,128)S(1)} %get-tuple-element.36), channel_id=1, source_target_pairs={{0,14},{2,0},{4,2},{6,4},{8,6},{10,8},{12,10},{14,12},{1,15},{3,1}... | collective-permute-start | bytes 1757192 | tf_op jit(solution)/shard_map/ppermute | solution.py:988
  34.4 13.1 %copy-start.4 = (f32[1,4,2]{1,2,0:T(2,128)S(1)}, f32[1,4,2]{1,2,0:T(2,128)}, u32[]{:S(2)}) copy-start(f32[1,4,2]{1,2,0:T(2,128)} %param.9) | copy-start | bytes 100
  34.4 18.3 %copy-start.1 = (s32[1,16,256]{2,1,0:T(8,128)S(1)}, s32[1,16,256]{2,1,0:T(8,128)}, u32[]{:S(2)}) copy-start(s32[1,16,256]{2,1,0:T(8,128)} %codes.1) | copy-start | bytes 49156
  34.4 18.3 %copy-start.2 = (s32[1,16,256]{2,1,0:T(8,128)S(1)}, s32[1,16,256]{2,1,0:T(8,128)}, u32[]{:S(2)}) copy-start(s32[1,16,256]{2,1,0:T(8,128)} %mask.1) | copy-start | bytes 49156
  45.4 7.3 %collective-permute-start.4 = (f32[8,16,256]{2,1,0:T(8,128)S(1)}, f32[8,16,256]{2,1,0:T(8,128)S(1)}, u32[]{:S(2)}, u32[]{:S(2)}) collective-permute-start(f32[8,16,256]{2,1,0:T(8,128)S(1)} %get-tuple-element.58), channel_id=1, source_target_pairs={{0,1},{1,0},{2,3},{3,2},{4,5},{5,4},{6,7},{7,6},{8,9},{9,8},{10,11... | collective-permute-start | bytes 393224 | tf_op jit(solution)/shard_map/ppermute | solution.py:995
  45.8 3.1 %collective-permute-start.5 = (f32[16,128]{1,0:T(8,128)S(1)}, f32[16,128]{1,0:T(8,128)S(1)}, u32[]{:S(2)}, u32[]{:S(2)}) collective-permute-start(f32[16,128]{1,0:T(8,128)S(1)} %get-tuple-element.59), channel_id=1, source_target_pairs={{0,17},{1,16},{16,33},{17,32},{32,49},{33,48},{48,65},{49,64},{64,... | collective-permute-start | bytes 24584 | tf_op jit(solution)/shard_map/ppermute | solution.py:1000
  46.3 6.4 %collective-permute-start.6 = (f32[16,128]{1,0:T(8,128)S(1)}, f32[16,128]{1,0:T(8,128)S(1)}, u32[]{:S(2)}, u32[]{:S(2)}) collective-permute-start(f32[16,128]{1,0:T(8,128)S(1)} %get-tuple-element.59), channel_id=1, source_target_pairs={{0,241},{1,240},{16,1},{17,0},{32,17},{33,16},{48,33},{49,32},{64,... | collective-permute-start | bytes 24584 | tf_op jit(solution)/shard_map/ppermute | solution.py:1001
